TPU v7x, 512 devices: a whole 4x8x8 slice. The times are simulated.
512 devices in a mesh: gx: 16 (over y, z_hi), gz: 32 (over x, z_lo, core).
Axes of the slice: x: 4, y: 8, z: 8 (z_hi: 2, z_lo: 4; z = z_hi * 4 + z_lo), core: 2. Of those that a mesh axis runs over, the one named last changes fastest.
Arguments:
- pressure: float32 [256, 512, 512], P('gx', 'gz'), may hold values from -6 to 6
- previous: float32 [256, 512, 512], P('gx', 'gz'), may hold values from -6 to 6
- states: float32 [16, 32, 256, 128], P('gx', 'gz'), may hold values from -4 to 4
- wall_cell: int32 [16, 32, 256], P('gx', 'gz'), may hold values from 0 to 131071, as said below
- wall_count: int32 [16, 32], P('gx', 'gz'), may hold values from 64 to 256, as said below
- material: int32 [16, 32, 256], P('gx', 'gz'), may hold values from 0 to 3
- partner: int32 [16, 32, 256], P('gx', 'gz'), may hold values from 0 to 1279
- transitions: float32 [4, 128, 128], replicated
- inputs: float32 [4, 128], replicated, may hold values from -4 to 4
- outputs: float32 [4, 128], replicated, may hold values from -0.5 to 0.5
Outputs:
- pressure_out: float32 [256, 512, 512], P('gx', 'gz')
- states_out: float32 [16, 32, 256, 128], P('gx', 'gz')
Inputs may be any that keep to these rules, and one draw needn't show every extreme that they name: `wall_cell`: within one device block the wall cells of all slots are distinct; slot k lies in the k-th of 256 equal runs of the block's flattened cells. `wall_count`: some device holds 256 live slots in every draw.
All inputs are finite; a program needn't handle non-finite values.
Results may differ from a plain program's by a relative error of at most 0.00026.
Values sent between devices are 32-bit elements; how exact they have to be, the bound alone decides.
A program may use at most 64 MiB of HBM per device.

v0:
```python
import jax
import jax.numpy as jnp
from jax import lax
from jax.sharding import PartitionSpec as P

STEPS = 3


face_w = 0.5
edge_w = 0.0625
corner_w = 0.0625
courant = 0.3
coupling = 0.3


def padded_2(value, sides, width):
    for axis, dim in sides:
        size, length = (lax.axis_size(axis), value.shape[dim])
        up = [(i, (i + 1) % size) for i in range(size - 1)]
        down = [(j, i) for i, j in up]
        last = lax.slice_in_dim(value, length - width, length, axis=dim)
        leading = lax.slice_in_dim(value, 0, width, axis=dim)
        before = lax.ppermute(last, axis, up)
        after = lax.ppermute(leading, axis, down)
        value = jnp.concatenate([before, value, after], axis=dim)
    return value


def shifted(block, axis, distance):
    devices = range(lax.axis_size(axis))
    route = [(i - distance, i) for i in devices if i - distance in devices]
    return lax.ppermute(block, axis, route)


def weight_of(first, second, third):
    count = abs(first) + abs(second) + abs(third)
    return [-(6 * face_w + 12 * edge_w + 8 * corner_w), face_w, edge_w, corner_w][count]


def laplace(padded, shape):
    total = jnp.zeros(shape, jnp.float32)
    for first in (-1, 0, 1):
        for second in (-1, 0, 1):
            for third in (-1, 0, 1):
                piece = padded[
                    1 + first : 1 + first + shape[0],
                    1 + second : 1 + second + shape[1],
                    1 + third : 1 + third + shape[2],
                ]
                total = total + weight_of(first, second, third) * piece
    return total


def extend(pressure):
    wider = padded_2(pressure, (("gx", 0), ("gz", 1)), 1)
    return jnp.pad(wider, ((0, 0), (0, 0), (1, 1)))


def exchange(pressure, state):
    lower_x = shifted(state, "gx", 1)
    upper_x = shifted(state, "gx", -1)
    lower_z = shifted(state, "gz", 1)
    upper_z = shifted(state, "gz", -1)
    found = jnp.concatenate([state, lower_x, upper_x, lower_z, upper_z], axis=0)
    return (extend(pressure), found)


def per_device(
    pressure,
    previous,
    states,
    wall_cell,
    wall_count,
    material,
    partner,
    transitions,
    inputs,
    outputs,
):
    highest = lax.Precision.HIGHEST
    shape = pressure.shape
    slots = states.shape[2]
    kinds = transitions.shape[0]
    cells = wall_cell.reshape(-1)
    livef = (jnp.arange(slots, dtype=jnp.int32) < wall_count[0, 0]).astype(jnp.float32)
    onehot = (material.reshape(-1)[:, None] == jnp.arange(kinds, dtype=jnp.int32)[None, :]).astype(
        jnp.float32
    )
    drive = jnp.dot(onehot, inputs, precision=highest)
    readout = jnp.dot(onehot, outputs, precision=highest)
    links = partner.reshape(-1)
    state = states.reshape(slots, -1) * livef[:, None]
    for step in range(STEPS):
        wider, found = exchange(pressure, state)
        lap = laplace(wider, shape)
        following = 2.0 * pressure - previous + courant * lap
        velocity = pressure.reshape(-1)[cells] - previous.reshape(-1)[cells]
        partner_state = jnp.take(found, links, axis=0)
        moved = jnp.einsum("wf,mfh->mwh", state, transitions, precision=highest)
        mixed = jnp.einsum("wm,mwh->wh", onehot, moved, precision=highest)
        new = (mixed + velocity[:, None] * drive + coupling * (partner_state - state)) * livef[
            :, None
        ]
        correction = jnp.sum(new * readout, axis=1) * livef
        following = following.reshape(-1).at[cells].add(-correction).reshape(shape)
        previous, pressure, state = (pressure, following, new)
    return (pressure, state.reshape(1, 1, slots, -1))


def solution(mesh):
    placed = (
        P("gx", "gz", None),
        P("gx", "gz", None),
        P("gx", "gz", None, None),
        P("gx", "gz", None),
        P("gx", "gz"),
        P("gx", "gz", None),
        P("gx", "gz", None),
        P(),
        P(),
        P(),
    )
    return jax.shard_map(
        per_device,
        mesh=mesh,
        in_specs=placed,
        out_specs=(P("gx", "gz", None), P("gx", "gz", None, None)),
        check_vma=False,
    )
```

profile of v0, /device:TPU:30, one launch (start us, length us, event | category | flops | bytes accessed | tf_op | source)
XLA Modules:
  0.0 200.6 jit_solution(3899642831431352865)
XLA Ops:
  4.3 7.6 %collective-permute-start.7 = (f32[256,128]{0,1:T(8,128)S(1)}, f32[256,128]{0,1:T(8,128)}, u32[]{:S(2)}, u32[]{:S(2)}) collective-permute-start(f32[256,128]{0,1:T(8,128)S(1)} %get-tuple-element.14), channel_id=1, source_target_pairs={{1,0},{2,1},{3,2},{4,3},{5,4},{6,5},{7,6},{8,7},{9,8},{10,9},{11,1... | collective-permute-start | bytes 393224 | tf_op jit(solution)/shard_map/ppermute | solution.py:32
  11.9 1.9 collective-permute-start.6
  13.8 8.1 %collective-permute-start.5 = (f32[256,128]{0,1:T(8,128)S(1)}, f32[256,128]{0,1:T(8,128)}, u32[]{:S(2)}, u32[]{:S(2)}) collective-permute-start(f32[256,128]{0,1:T(8,128)S(1)} %get-tuple-element.14), channel_id=1, source_target_pairs={{32,0},{64,32},{96,64},{128,96},{160,128},{192,160},{224,192},{256... | collective-permute-start | bytes 393224 | tf_op jit(solution)/shard_map/ppermute | solution.py:32
  24.6 7.8 %collective-permute-start = (f32[1,16,512]{2,1,0:T(8,128)S(1)}, f32[1,16,512]{2,1,0:T(8,128)S(1)}, u32[]{:S(2)}, u32[]{:S(2)}) collective-permute-start(f32[1,16,512]{2,1,0:T(8,128)S(1)} %get-tuple-element.26), channel_id=1, source_target_pairs={{0,32},{32,64},{64,96},{96,128},{128,160},{160,192},{192,224},{224... | collective-permute-start | bytes 98312 | tf_op jit(solution)/shard_map/ppermute | solution.py:23
  40.3 6.3 %collective-permute-start.3 = (f32[18,1,512]{2,1,0:T(1,128)S(1)}, f32[18,1,512]{2,1,0:T(1,128)S(1)}, u32[]{:S(2)}, u32[]{:S(2)}) collective-permute-start(f32[18,1,512]{2,1,0:T(1,128)S(1)} %get-tuple-element.20), channel_id=1, source_target_pairs={{1,0},{2,1},{3,2},{4,3},{5,4},{6,5},{7,6},{8,7},{9,8},{10,9},{11,1... | collective-permute-start | bytes 110600 | tf_op jit(solution)/shard_map/ppermute | solution.py:24
  47.5 2.5 %gather_fusion = f32[256]{0:T(256)} fusion(f32[131072]{0:T(1024)S(1)} %bitcast.75, s32[1024]{0:T(1024)} %pad_clamp_fusion.1), kind=kCustom, calls=%fused_computation.3 | custom fusion | bytes 3072 | tf_op jit(solution)/shard_map/gather | solution.py:97
  50.0 2.0 gather_fusion.1
  52.1 4.1 %collective-permute-start.4 = (f32[256,128]{0,1:T(8,128)S(1)}, f32[256,128]{0,1:T(8,128)S(1)}, u32[]{:S(2)}, u32[]{:S(2)}) collective-permute-start(f32[256,128]{0,1:T(8,128)S(1)} %get-tuple-element.14), channel_id=1, source_target_pairs={{0,32},{32,64},{64,96},{96,128},{128,160},{160,192},{192,224},{224... | collective-permute-start | bytes 393224 | tf_op jit(solution)/shard_map/ppermute | solution.py:32
  56.9 2.4 %fusion.87 = f32[16,16,512]{2,1,0:T(8,128)S(1)} fusion(f32[18,16,512]{2,1,0:T(8,128)S(1)} %constant_dynamic-update-slice_fusion, f32[18,1,512]{2,1,0:T(1,128)S(1)} %collective-permute-done.3, f32[18,1,512]{2,1,0:T(1,128)S(1)} %collective-permute-done.2, f32[18,18,514]{2,1,0:T(8,128)S(1)} %select_maximum_fusion.4, ...), kind=kLoop, calls=%fused_computation.129 | loop fusion | flops 8126464 | bytes 11739136 | tf_op jit(solution)/shard_map/add | solution.py:96
  59.5 4.3 %collective-permute-done.4 = f32[256,128]{0,1:T(8,128)S(1)} collective-permute-done((f32[256,128]{0,1:T(8,128)S(1)}, f32[256,128]{0,1:T(8,128)S(1)}, u32[]{:S(2)}, u32[]{:S(2)}) %collective-permute-start.4) | collective-permute-done | bytes 131104 | tf_op jit(solution)/shard_map/ppermute | solution.py:32
  72.4 2.3 %collective-permute-start.15 = (f32[256,128]{0,1:T(8,128)S(1)}, f32[256,128]{0,1:T(8,128)S(1)}, u32[]{:S(2)}, u32[]{:S(2)}) collective-permute-start(f32[256,128]{0,1:T(8,128)S(1)} %get-tuple-element.12), channel_id=1, source_target_pairs={{1,0},{2,1},{3,2},{4,3},{5,4},{6,5},{7,6},{8,7},{9,8},{10,9},{11,1... | collective-permute-start | bytes 393224 | tf_op jit(solution)/shard_map/ppermute | solution.py:32
  74.8 2.0 collective-permute-start.14
  76.8 4.9 %collective-permute-start.13 = (f32[256,128]{0,1:T(8,128)S(1)}, f32[256,128]{0,1:T(8,128)S(1)}, u32[]{:S(2)}, u32[]{:S(2)}) collective-permute-start(f32[256,128]{0,1:T(8,128)S(1)} %get-tuple-element.12), channel_id=1, source_target_pairs={{32,0},{64,32},{96,64},{128,96},{160,128},{192,160},{224,192},{256... | collective-permute-start | bytes 393224 | tf_op jit(solution)/shard_map/ppermute | solution.py:32
  82.0 2.2 %scatter_fusion = f32[131072]{0:T(1024)S(1)} fusion(f32[131072]{0:T(1024)S(1)} %bitcast.70, s32[256]{0:T(256)S(1)} %bitcast.82, f32[256]{0:T(256)S(1)} %select_negate_fusion.2), kind=kCustom, calls=%fused_computation.7 | custom fusion | flops 256 | bytes 4096 | tf_op jit(solution)/shard_map/scatter-add | solution.py:105
  84.2 4.9 %collective-permute-start.8 = (f32[1,16,512]{2,1,0:T(8,128)S(1)}, f32[1,16,512]{2,1,0:T(8,128)S(1)}, u32[]{:S(2)}, u32[]{:S(2)}) collective-permute-start(f32[1,16,512]{2,1,0:T(8,128)S(1)} %slice.408), channel_id=1, source_target_pairs={{0,32},{32,64},{64,96},{96,128},{128,160},{160,192},{192,224},{224... | collective-permute-start | bytes 98312 | tf_op jit(solution)/shard_map/ppermute | solution.py:23
  90.6 5.9 %collective-permute-start.9 = (f32[1,16,512]{2,1,0:T(8,128)S(1)}, f32[1,16,512]{2,1,0:T(8,128)S(1)}, u32[]{:S(2)}, u32[]{:S(2)}) collective-permute-start(f32[1,16,512]{2,1,0:T(8,128)S(1)} %slice.410), channel_id=1, source_target_pairs={{32,0},{64,32},{96,64},{128,96},{160,128},{192,160},{224,192},{256... | collective-permute-start | bytes 98312 | tf_op jit(solution)/shard_map/ppermute | solution.py:24
  96.6 4.1 %collective-permute-done.9 = f32[1,16,512]{2,1,0:T(8,128)S(1)} collective-permute-done((f32[1,16,512]{2,1,0:T(8,128)S(1)}, f32[1,16,512]{2,1,0:T(8,128)S(1)}, u32[]{:S(2)}, u32[]{:S(2)}) %collective-permute-start.9) | collective-permute-done | bytes 32800 | tf_op jit(solution)/shard_map/ppermute | solution.py:24
  102.7 6.3 %collective-permute-start.11 = (f32[18,1,512]{2,1,0:T(1,128)S(1)}, f32[18,1,512]{2,1,0:T(1,128)S(1)}, u32[]{:S(2)}, u32[]{:S(2)}) collective-permute-start(f32[18,1,512]{2,1,0:T(1,128)S(1)} %get-tuple-element.18), channel_id=1, source_target_pairs={{1,0},{2,1},{3,2},{4,3},{5,4},{6,5},{7,6},{8,7},{9,8},{10,9},{11,1... | collective-permute-start | bytes 110600 | tf_op jit(solution)/shard_map/ppermute | solution.py:24
  111.0 2.5 %gather_fusion.2 = f32[256]{0:T(256)} fusion(f32[131072]{0:T(1024)S(1)} %scatter_fusion, s32[1024]{0:T(1024)} %pad_clamp_fusion.1), kind=kCustom, calls=%fused_computation.5 | custom fusion | bytes 3072 | tf_op jit(solution)/shard_map/gather | solution.py:97
  115.7 10.1 %collective-permute-start.12 = (f32[256,128]{0,1:T(8,128)S(1)}, f32[256,128]{0,1:T(8,128)S(1)}, u32[]{:S(2)}, u32[]{:S(2)}) collective-permute-start(f32[256,128]{0,1:T(8,128)S(1)} %get-tuple-element.12), channel_id=1, source_target_pairs={{0,32},{32,64},{64,96},{96,128},{128,160},{160,192},{192,224},{224... | collective-permute-start | bytes 393224 | tf_op jit(solution)/shard_map/ppermute | solution.py:32
  126.4 2.4 %fusion.51 = f32[16,16,512]{2,1,0:T(8,128)S(1)} fusion(f32[18,16,512]{2,1,0:T(8,128)S(1)} %constant_dynamic-update-slice_fusion.8, f32[18,1,512]{2,1,0:T(1,128)S(1)} %collective-permute-done.11, f32[18,1,512]{2,1,0:T(1,128)S(1)} %collective-permute-done.10, f32[18,18,514]{2,1,0:T(8,128)S(1)} %select_maximum_fusion.2, ...), kind=kLoop, calls=%fused_computation.93 | loop fusion | flops 8126464 | bytes 11739136 | tf_op jit(solution)/shard_map/add | solution.py:96
  134.9 2.1 %collective-permute-start.23 = (f32[256,128]{0,1:T(8,128)S(1)}, f32[256,128]{0,1:T(8,128)S(1)}, u32[]{:S(2)}, u32[]{:S(2)}) collective-permute-start(f32[256,128]{0,1:T(8,128)S(1)} %get-tuple-element.10), channel_id=1, source_target_pairs={{1,0},{2,1},{3,2},{4,3},{5,4},{6,5},{7,6},{8,7},{9,8},{10,9},{11,1... | collective-permute-start | bytes 393224 | tf_op jit(solution)/shard_map/ppermute | solution.py:32
  137.0 2.2 %collective-permute-start.22 = (f32[256,128]{0,1:T(8,128)S(1)}, f32[256,128]{0,1:T(8,128)S(1)}, u32[]{:S(2)}, u32[]{:S(2)}) collective-permute-start(f32[256,128]{0,1:T(8,128)S(1)} %get-tuple-element.10), channel_id=1, source_target_pairs={{0,1},{1,2},{2,3},{3,4},{4,5},{5,6},{6,7},{7,8},{8,9},{9,10},{10,1... | collective-permute-start | bytes 393224 | tf_op jit(solution)/shard_map/ppermute | solution.py:32
  139.2 3.8 %collective-permute-start.21 = (f32[256,128]{0,1:T(8,128)S(1)}, f32[256,128]{0,1:T(8,128)S(1)}, u32[]{:S(2)}, u32[]{:S(2)}) collective-permute-start(f32[256,128]{0,1:T(8,128)S(1)} %get-tuple-element.10), channel_id=1, source_target_pairs={{32,0},{64,32},{96,64},{128,96},{160,128},{192,160},{224,192},{256... | collective-permute-start | bytes 393224 | tf_op jit(solution)/shard_map/ppermute | solution.py:32
  143.1 2.2 %scatter_fusion.1 = f32[131072]{0:T(1024)S(1)} fusion(f32[131072]{0:T(1024)S(1)} %bitcast.71, s32[256]{0:T(256)S(1)} %bitcast.83, f32[256]{0:T(256)S(1)} %select_negate_fusion.1), kind=kCustom, calls=%fused_computation.8 | custom fusion | flops 256 | bytes 4096 | tf_op jit(solution)/shard_map/scatter-add | solution.py:105
  145.3 5.9 %collective-permute-start.16 = (f32[1,16,512]{2,1,0:T(8,128)S(1)}, f32[1,16,512]{2,1,0:T(8,128)S(1)}, u32[]{:S(2)}, u32[]{:S(2)}) collective-permute-start(f32[1,16,512]{2,1,0:T(8,128)S(1)} %slice.440), channel_id=1, source_target_pairs={{0,32},{32,64},{64,96},{96,128},{128,160},{160,192},{192,224},{224... | collective-permute-start | bytes 98312 | tf_op jit(solution)/shard_map/ppermute | solution.py:23
  152.8 4.9 %collective-permute-start.17 = (f32[1,16,512]{2,1,0:T(8,128)S(1)}, f32[1,16,512]{2,1,0:T(8,128)S(1)}, u32[]{:S(2)}, u32[]{:S(2)}) collective-permute-start(f32[1,16,512]{2,1,0:T(8,128)S(1)} %slice.442), channel_id=1, source_target_pairs={{32,0},{64,32},{96,64},{128,96},{160,128},{192,160},{224,192},{256... | collective-permute-start | bytes 98312 | tf_op jit(solution)/shard_map/ppermute | solution.py:24
  157.7 6.5 %collective-permute-done.17 = f32[1,16,512]{2,1,0:T(8,128)S(1)} collective-permute-done((f32[1,16,512]{2,1,0:T(8,128)S(1)}, f32[1,16,512]{2,1,0:T(8,128)S(1)}, u32[]{:S(2)}, u32[]{:S(2)}) %collective-permute-start.17) | collective-permute-done | bytes 32800 | tf_op jit(solution)/shard_map/ppermute | solution.py:24
  166.8 6.3 %collective-permute-start.19 = (f32[18,1,512]{2,1,0:T(1,128)S(1)}, f32[18,1,512]{2,1,0:T(1,128)S(1)}, u32[]{:S(2)}, u32[]{:S(2)}) collective-permute-start(f32[18,1,512]{2,1,0:T(1,128)S(1)} %get-tuple-element.16), channel_id=1, source_target_pairs={{1,0},{2,1},{3,2},{4,3},{5,4},{6,5},{7,6},{8,7},{9,8},{10,9},{11,1... | collective-permute-start | bytes 110600 | tf_op jit(solution)/shard_map/ppermute | solution.py:24
  178.5 9.9 %collective-permute-start.20 = (f32[256,128]{0,1:T(8,128)S(1)}, f32[256,128]{0,1:T(8,128)S(1)}, u32[]{:S(2)}, u32[]{:S(2)}) collective-permute-start(f32[256,128]{0,1:T(8,128)S(1)} %get-tuple-element.10), channel_id=1, source_target_pairs={{0,32},{32,64},{64,96},{96,128},{128,160},{160,192},{192,224},{224... | collective-permute-start | bytes 393224 | tf_op jit(solution)/shard_map/ppermute | solution.py:32
  189.1 2.4 %fusion.15 = f32[16,16,512]{2,1,0:T(8,128)S(1)} fusion(f32[18,16,512]{2,1,0:T(8,128)S(1)} %constant_dynamic-update-slice_fusion.16, f32[18,1,512]{2,1,0:T(1,128)S(1)} %collective-permute-done.19, f32[18,1,512]{2,1,0:T(1,128)S(1)} %collective-permute-done.18, f32[18,18,514]{2,1,0:T(8,128)S(1)} %select_maximum_fusion, ...), kind=kLoop, calls=%fused_computation.57 | loop fusion | flops 8126464 | bytes 11739136 | tf_op jit(solution)/shard_map/add | solution.py:96
  197.6 2.2 %scatter_fusion.2 = f32[131072]{0:T(1024)S(1)} fusion(f32[131072]{0:T(1024)S(1)} %bitcast.73, s32[256]{0:T(256)S(1)} %bitcast.84, f32[256]{0:T(256)S(1)} %select_negate_fusion), kind=kCustom, calls=%fused_computation.9 | custom fusion | flops 256 | bytes 4096 | tf_op jit(solution)/shard_map/scatter-add | solution.py:105
  (153 shorter events, 55.1 us)
Async XLA Ops:
  0.6 35.0 %copy-start = (f32[4,128,128]{2,1,0:T(8,128)S(1)}, f32[4,128,128]{2,1,0:T(8,128)}, u32[]{:S(2)}) copy-start(f32[4,128,128]{2,1,0:T(8,128)} %param.19) | copy-start | bytes 786436
  3.6 32.0 %copy-start.11 = (f32[256]{0:T(256)}, f32[256]{0:T(256)S(1)}, u32[]{:S(2)}) copy-start(f32[256]{0:T(256)S(1)} %get-tuple-element.30) | copy-start | bytes 3076
  4.3 63.3 %collective-permute-start.7 = (f32[256,128]{0,1:T(8,128)S(1)}, f32[256,128]{0,1:T(8,128)}, u32[]{:S(2)}, u32[]{:S(2)}) collective-permute-start(f32[256,128]{0,1:T(8,128)S(1)} %get-tuple-element.14), channel_id=1, source_target_pairs={{1,0},{2,1},{3,2},{4,3},{5,4},{6,5},{7,6},{8,7},{9,8},{10,9},{11,1... | collective-permute-start | bytes 393224 | tf_op jit(solution)/shard_map/ppermute | solution.py:32
  11.9 54.2 %collective-permute-start.6 = (f32[256,128]{0,1:T(8,128)S(1)}, f32[256,128]{0,1:T(8,128)}, u32[]{:S(2)}, u32[]{:S(2)}) collective-permute-start(f32[256,128]{0,1:T(8,128)S(1)} %get-tuple-element.14), channel_id=1, source_target_pairs={{0,1},{1,2},{2,3},{3,4},{4,5},{5,6},{6,7},{7,8},{8,9},{9,10},{10,1... | collective-permute-start | bytes 393224 | tf_op jit(solution)/shard_map/ppermute | solution.py:32
  13.8 50.6 %collective-permute-start.5 = (f32[256,128]{0,1:T(8,128)S(1)}, f32[256,128]{0,1:T(8,128)}, u32[]{:S(2)}, u32[]{:S(2)}) collective-permute-start(f32[256,128]{0,1:T(8,128)S(1)} %get-tuple-element.14), channel_id=1, source_target_pairs={{32,0},{64,32},{96,64},{128,96},{160,128},{192,160},{224,192},{256... | collective-permute-start | bytes 393224 | tf_op jit(solution)/shard_map/ppermute | solution.py:32
  22.7 15.5 %collective-permute-start.1 = (f32[1,16,512]{2,1,0:T(8,128)S(1)}, f32[1,16,512]{2,1,0:T(8,128)S(1)}, u32[]{:S(2)}, u32[]{:S(2)}) collective-permute-start(f32[1,16,512]{2,1,0:T(8,128)S(1)} %get-tuple-element.25), channel_id=1, source_target_pairs={{32,0},{64,32},{96,64},{128,96},{160,128},{192,160},{224,192},{256... | collective-permute-start | bytes 98312 | tf_op jit(solution)/shard_map/ppermute | solution.py:24
  24.6 13.5 %collective-permute-start = (f32[1,16,512]{2,1,0:T(8,128)S(1)}, f32[1,16,512]{2,1,0:T(8,128)S(1)}, u32[]{:S(2)}, u32[]{:S(2)}) collective-permute-start(f32[1,16,512]{2,1,0:T(8,128)S(1)} %get-tuple-element.26), channel_id=1, source_target_pairs={{0,32},{32,64},{64,96},{96,128},{128,160},{160,192},{192,224},{224... | collective-permute-start | bytes 98312 | tf_op jit(solution)/shard_map/ppermute | solution.py:23
  33.8 12.8 %copy-start.8 = (s32[256,1]{0,1:T(1,128)}, s32[256,1]{0,1:T(1,128)S(1)}, u32[]{:S(2)}) copy-start(s32[256,1]{0,1:T(1,128)S(1)} %compare_select_fusion) | copy-start | bytes 3076
  38.3 13.8 %collective-permute-start.2 = (f32[18,1,512]{2,1,0:T(1,128)S(1)}, f32[18,1,512]{2,1,0:T(1,128)S(1)}, u32[]{:S(2)}, u32[]{:S(2)}) collective-permute-start(f32[18,1,512]{2,1,0:T(1,128)S(1)} %get-tuple-element.19), channel_id=1, source_target_pairs={{0,1},{1,2},{2,3},{3,4},{4,5},{5,6},{6,7},{7,8},{8,9},{9,10},{10,1... | collective-permute-start | bytes 110600 | tf_op jit(solution)/shard_map/ppermute | solution.py:23
  40.3 16.0 %collective-permute-start.3 = (f32[18,1,512]{2,1,0:T(1,128)S(1)}, f32[18,1,512]{2,1,0:T(1,128)S(1)}, u32[]{:S(2)}, u32[]{:S(2)}) collective-permute-start(f32[18,1,512]{2,1,0:T(1,128)S(1)} %get-tuple-element.20), channel_id=1, source_target_pairs={{1,0},{2,1},{3,2},{4,3},{5,4},{6,5},{7,6},{8,7},{9,8},{10,9},{11,1... | collective-permute-start | bytes 110600 | tf_op jit(solution)/shard_map/ppermute | solution.py:24
  52.1 11.7 %collective-permute-start.4 = (f32[256,128]{0,1:T(8,128)S(1)}, f32[256,128]{0,1:T(8,128)S(1)}, u32[]{:S(2)}, u32[]{:S(2)}) collective-permute-start(f32[256,128]{0,1:T(8,128)S(1)} %get-tuple-element.14), channel_id=1, source_target_pairs={{0,32},{32,64},{64,96},{96,128},{128,160},{160,192},{192,224},{224... | collective-permute-start | bytes 393224 | tf_op jit(solution)/shard_map/ppermute | solution.py:32
  70.6 11.4 %copy-start.9 = (s32[256,1]{0,1:T(1,128)S(1)}, s32[256,1]{0,1:T(1,128)}, u32[]{:S(2)}) copy-start(s32[256,1]{0,1:T(1,128)} %copy-done.8) | copy-start | bytes 3076
  72.4 58.7 %collective-permute-start.15 = (f32[256,128]{0,1:T(8,128)S(1)}, f32[256,128]{0,1:T(8,128)S(1)}, u32[]{:S(2)}, u32[]{:S(2)}) collective-permute-start(f32[256,128]{0,1:T(8,128)S(1)} %get-tuple-element.12), channel_id=1, source_target_pairs={{1,0},{2,1},{3,2},{4,3},{5,4},{6,5},{7,6},{8,7},{9,8},{10,9},{11,1... | collective-permute-start | bytes 393224 | tf_op jit(solution)/shard_map/ppermute | solution.py:32
  74.8 55.7 %collective-permute-start.14 = (f32[256,128]{0,1:T(8,128)S(1)}, f32[256,128]{0,1:T(8,128)S(1)}, u32[]{:S(2)}, u32[]{:S(2)}) collective-permute-start(f32[256,128]{0,1:T(8,128)S(1)} %get-tuple-element.12), channel_id=1, source_target_pairs={{0,1},{1,2},{2,3},{3,4},{4,5},{5,6},{6,7},{7,8},{8,9},{9,10},{10,1... | collective-permute-start | bytes 393224 | tf_op jit(solution)/shard_map/ppermute | solution.py:32
  76.8 53.0 %collective-permute-start.13 = (f32[256,128]{0,1:T(8,128)S(1)}, f32[256,128]{0,1:T(8,128)S(1)}, u32[]{:S(2)}, u32[]{:S(2)}) collective-permute-start(f32[256,128]{0,1:T(8,128)S(1)} %get-tuple-element.12), channel_id=1, source_target_pairs={{32,0},{64,32},{96,64},{128,96},{160,128},{192,160},{224,192},{256... | collective-permute-start | bytes 393224 | tf_op jit(solution)/shard_map/ppermute | solution.py:32
  84.2 12.3 %collective-permute-start.8 = (f32[1,16,512]{2,1,0:T(8,128)S(1)}, f32[1,16,512]{2,1,0:T(8,128)S(1)}, u32[]{:S(2)}, u32[]{:S(2)}) collective-permute-start(f32[1,16,512]{2,1,0:T(8,128)S(1)} %slice.408), channel_id=1, source_target_pairs={{0,32},{32,64},{64,96},{96,128},{128,160},{160,192},{192,224},{224... | collective-permute-start | bytes 98312 | tf_op jit(solution)/shard_map/ppermute | solution.py:23
  90.5 18.6 %copy-start.6 = (pred[256,4,1]{1,0,2:T(32,128)(4,1)S(1)}, pred[256,4,1]{1,0,2:T(32,128)(4,1)}, u32[]{:S(2)}) copy-start(pred[256,4,1]{1,0,2:T(32,128)(4,1)} %copy-done.5) | copy-start | bytes 3076
  90.6 18.5 %copy-start.4 = (f32[256,4,128]{2,0,1:T(8,128)S(1)}, f32[256,4,128]{2,0,1:T(8,128)}, u32[]{:S(2)}) copy-start(f32[256,4,128]{2,0,1:T(8,128)} %fusion.139) | copy-start | bytes 1572868
  90.6 10.1 %collective-permute-start.9 = (f32[1,16,512]{2,1,0:T(8,128)S(1)}, f32[1,16,512]{2,1,0:T(8,128)S(1)}, u32[]{:S(2)}, u32[]{:S(2)}) collective-permute-start(f32[1,16,512]{2,1,0:T(8,128)S(1)} %slice.410), channel_id=1, source_target_pairs={{32,0},{64,32},{96,64},{128,96},{160,128},{192,160},{224,192},{256... | collective-permute-start | bytes 98312 | tf_op jit(solution)/shard_map/ppermute | solution.py:24
  100.8 14.9 %collective-permute-start.10 = (f32[18,1,512]{2,1,0:T(1,128)S(1)}, f32[18,1,512]{2,1,0:T(1,128)S(1)}, u32[]{:S(2)}, u32[]{:S(2)}) collective-permute-start(f32[18,1,512]{2,1,0:T(1,128)S(1)} %get-tuple-element.17), channel_id=1, source_target_pairs={{0,1},{1,2},{2,3},{3,4},{4,5},{5,6},{6,7},{7,8},{8,9},{9,10},{10,1... | collective-permute-start | bytes 110600 | tf_op jit(solution)/shard_map/ppermute | solution.py:23
  102.7 23.1 %collective-permute-start.11 = (f32[18,1,512]{2,1,0:T(1,128)S(1)}, f32[18,1,512]{2,1,0:T(1,128)S(1)}, u32[]{:S(2)}, u32[]{:S(2)}) collective-permute-start(f32[18,1,512]{2,1,0:T(1,128)S(1)} %get-tuple-element.18), channel_id=1, source_target_pairs={{1,0},{2,1},{3,2},{4,3},{5,4},{6,5},{7,6},{8,7},{9,8},{10,9},{11,1... | collective-permute-start | bytes 110600 | tf_op jit(solution)/shard_map/ppermute | solution.py:24
  115.7 13.3 %collective-permute-start.12 = (f32[256,128]{0,1:T(8,128)S(1)}, f32[256,128]{0,1:T(8,128)S(1)}, u32[]{:S(2)}, u32[]{:S(2)}) collective-permute-start(f32[256,128]{0,1:T(8,128)S(1)} %get-tuple-element.12), channel_id=1, source_target_pairs={{0,32},{32,64},{64,96},{96,128},{128,160},{160,192},{192,224},{224... | collective-permute-start | bytes 393224 | tf_op jit(solution)/shard_map/ppermute | solution.py:32
  134.9 58.8 %collective-permute-start.23 = (f32[256,128]{0,1:T(8,128)S(1)}, f32[256,128]{0,1:T(8,128)S(1)}, u32[]{:S(2)}, u32[]{:S(2)}) collective-permute-start(f32[256,128]{0,1:T(8,128)S(1)} %get-tuple-element.10), channel_id=1, source_target_pairs={{1,0},{2,1},{3,2},{4,3},{5,4},{6,5},{7,6},{8,7},{9,8},{10,9},{11,1... | collective-permute-start | bytes 393224 | tf_op jit(solution)/shard_map/ppermute | solution.py:32
  137.0 56.1 %collective-permute-start.22 = (f32[256,128]{0,1:T(8,128)S(1)}, f32[256,128]{0,1:T(8,128)S(1)}, u32[]{:S(2)}, u32[]{:S(2)}) collective-permute-start(f32[256,128]{0,1:T(8,128)S(1)} %get-tuple-element.10), channel_id=1, source_target_pairs={{0,1},{1,2},{2,3},{3,4},{4,5},{5,6},{6,7},{7,8},{8,9},{9,10},{10,1... | collective-permute-start | bytes 393224 | tf_op jit(solution)/shard_map/ppermute | solution.py:32
  139.2 53.2 %collective-permute-start.21 = (f32[256,128]{0,1:T(8,128)S(1)}, f32[256,128]{0,1:T(8,128)S(1)}, u32[]{:S(2)}, u32[]{:S(2)}) collective-permute-start(f32[256,128]{0,1:T(8,128)S(1)} %get-tuple-element.10), channel_id=1, source_target_pairs={{32,0},{64,32},{96,64},{128,96},{160,128},{192,160},{224,192},{256... | collective-permute-start | bytes 393224 | tf_op jit(solution)/shard_map/ppermute | solution.py:32
  145.3 12.3 %collective-permute-start.16 = (f32[1,16,512]{2,1,0:T(8,128)S(1)}, f32[1,16,512]{2,1,0:T(8,128)S(1)}, u32[]{:S(2)}, u32[]{:S(2)}) collective-permute-start(f32[1,16,512]{2,1,0:T(8,128)S(1)} %slice.440), channel_id=1, source_target_pairs={{0,32},{32,64},{64,96},{96,128},{128,160},{160,192},{192,224},{224... | collective-permute-start | bytes 98312 | tf_op jit(solution)/shard_map/ppermute | solution.py:23
  152.6 20.5 %copy-start.7 = (pred[256,4,1]{1,0,2:T(32,128)(4,1)S(1)}, pred[256,4,1]{1,0,2:T(32,128)(4,1)}, u32[]{:S(2)}) copy-start(pred[256,4,1]{1,0,2:T(32,128)(4,1)} %copy-done.5) | copy-start | bytes 3076
  152.7 20.4 %copy-start.3 = (f32[256,4,128]{2,0,1:T(8,128)S(1)}, f32[256,4,128]{2,0,1:T(8,128)}, u32[]{:S(2)}) copy-start(f32[256,4,128]{2,0,1:T(8,128)} %fusion.135) | copy-start | bytes 1572868
  152.8 11.5 %collective-permute-start.17 = (f32[1,16,512]{2,1,0:T(8,128)S(1)}, f32[1,16,512]{2,1,0:T(8,128)S(1)}, u32[]{:S(2)}, u32[]{:S(2)}) collective-permute-start(f32[1,16,512]{2,1,0:T(8,128)S(1)} %slice.442), channel_id=1, source_target_pairs={{32,0},{64,32},{96,64},{128,96},{160,128},{192,160},{224,192},{256... | collective-permute-start | bytes 98312 | tf_op jit(solution)/shard_map/ppermute | solution.py:24
  164.9 13.6 %collective-permute-start.18 = (f32[18,1,512]{2,1,0:T(1,128)}, f32[18,1,512]{2,1,0:T(1,128)S(1)}, u32[]{:S(2)}, u32[]{:S(2)}) collective-permute-start(f32[18,1,512]{2,1,0:T(1,128)} %get-tuple-element.15), channel_id=1, source_target_pairs={{0,1},{1,2},{2,3},{3,4},{4,5},{5,6},{6,7},{7,8},{8,9},{9,10},{10,1... | collective-permute-start | bytes 110600 | tf_op jit(solution)/shard_map/ppermute | solution.py:23
  166.8 21.6 %collective-permute-start.19 = (f32[18,1,512]{2,1,0:T(1,128)S(1)}, f32[18,1,512]{2,1,0:T(1,128)S(1)}, u32[]{:S(2)}, u32[]{:S(2)}) collective-permute-start(f32[18,1,512]{2,1,0:T(1,128)S(1)} %get-tuple-element.16), channel_id=1, source_target_pairs={{1,0},{2,1},{3,2},{4,3},{5,4},{6,5},{7,6},{8,7},{9,8},{10,9},{11,1... | collective-permute-start | bytes 110600 | tf_op jit(solution)/shard_map/ppermute | solution.py:24
  178.5 13.1 %collective-permute-start.20 = (f32[256,128]{0,1:T(8,128)S(1)}, f32[256,128]{0,1:T(8,128)S(1)}, u32[]{:S(2)}, u32[]{:S(2)}) collective-permute-start(f32[256,128]{0,1:T(8,128)S(1)} %get-tuple-element.10), channel_id=1, source_target_pairs={{0,32},{32,64},{64,96},{96,128},{128,160},{160,192},{192,224},{224... | collective-permute-start | bytes 393224 | tf_op jit(solution)/shard_map/ppermute | solution.py:32
  (15 other events, 76.5 us)
where the time goes:
time: 202 us; the launch traced here: 201 us
  starting transfers between devices  115 us (57%)
  local copies, waits for them, and re-layouts  34.2 us (17%)
  other arithmetic  24.2 us (12%)
  waiting for transfers between devices  15 us (7%)
  matrix products  9.79 us (5%)
  between operations  2.25 us (1%)
    ppermute x12, starting transfers between devices, shifted(): return lax.ppermute(block, axis, route)  59.2 us
    ppermute x6, starting transfers between devices, padded_2(): after = lax.ppermute(leading, axis, down)  31.7 us
    ppermute x6, starting transfers between devices, padded_2(): before = lax.ppermute(last, axis, up)  24.3 us
    ppermute x6, waiting for transfers between devices, padded_2(): after = lax.ppermute(leading, axis, down)  10.6 us
    unnamed x68, local copies, waits for them, and re-layouts  10.6 us
    gather x4, local copies, waits for them, and re-layouts, per_device(): velocity = pressure.reshape(-1)[cells] - previous.reshape(-1)[cells]  8.79 us
    add x3, other arithmetic, per_device(): following = 2.0 * pressure - previous + courant * lap  7.33 us
    concatenate x6, local copies, waits for them, and re-layouts, exchange(): found = jnp.concatenate([state, lower_x, upper_x, lower_z, upper_z], axis=0)  7.04 us
  transfers between devices with their start and end apart: 24, of which 3 were waited for; matrix products, arithmetic and copies ran while one was open for 25% of the time, Pallas kernels for 0%

commit v1 on v0

v1 whole, which is shorter than its diff:
```python
import functools

import jax
import jax.numpy as jnp
from jax import lax
from jax.experimental import pallas as pl
from jax.experimental.pallas import tpu as pltpu
from jax.sharding import PartitionSpec as P

MESH = pl.DeviceIdType.MESH
STEPS = 3
CHUNKS = 4
MIRROR, OTHER, BEFORE, AFTER = range(4)

face_w = 0.5
edge_w = 0.0625
corner_w = 0.0625
centre_w = -(6 * face_w + 12 * edge_w + 8 * corner_w)
courant = 0.3
coupling = 0.3


def split(value):
    high = value.astype(jnp.bfloat16)
    low = (value - high.astype(jnp.float32)).astype(jnp.bfloat16)
    return high, low


def dot(left, right):
    return jnp.dot(left, right, preferred_element_type=jnp.float32)


def kernel(
    sizes,
    p_ref,
    q_ref,
    s_ref,
    cell_ref,
    count_ref,
    material_ref,
    partner_ref,
    transition_ref,
    input_ref,
    output_ref,
    p_out,
    s_out,
    state,
    found,
    gather,
    mix_a,
    mix_b,
    drive,
    readout,
    mask,
    p_mid,
    halo_x,
    halo_z,
    halo_c,
    face_z,
    face_c,
    beside,
    free,
    picked,
    s_send,
    s_recv,
    p_send,
    p_recv,
):
    n_gx, n_gz = sizes
    cx, cz, ny = p_ref.shape
    slots, filt = s_ref.shape
    kinds = transition_ref.shape[0]
    rows = filt // CHUNKS
    lanes = 128
    i, j = lax.axis_index("gx"), lax.axis_index("gz")
    upper = lax.rem(i, 2)
    has_xm, has_xp = i > 0, i < n_gx - 1
    has_zm, has_zp = j > 0, j < n_gz - 1
    mirror = (i + 1 - 2 * upper, j)
    relay_to = (i + 2 - 4 * upper, j)
    has_mirror = jnp.logical_or(upper == 1, has_xp)
    other_at = i - 1 + 2 * upper
    has_other = jnp.logical_and(other_at >= 0, other_at < n_gx)
    can_relay = jnp.logical_and(
        jnp.logical_and(relay_to[0] >= 0, relay_to[0] < n_gx), has_mirror
    )

    near = {}
    for dx in (-1, 0, 1):
        for dz in (-1, 0, 1):
            if dx or dz:
                present = [has_xm, None, has_xp][dx + 1], [has_zm, None, has_zp][dz + 1]
                present = [one for one in present if one is not None]
                near[dx, dz] = (functools.reduce(jnp.logical_and, present), (i + dx, j + dz))
    greeted = list(near.values()) + [(i >= 2, (i - 2, j)), (i < n_gx - 2, (i + 2, j))]

    barrier = pltpu.get_barrier_semaphore()
    for present, device in greeted:

        @pl.when(present)
        def _():
            pl.semaphore_signal(barrier, inc=1, device_id=device, device_id_type=MESH)

    state[0] = jnp.transpose(s_ref[...]) * (
        lax.broadcasted_iota(jnp.int32, (filt, slots), 1) < count_ref[0, 0]
    ).astype(jnp.float32)
    live = (lax.broadcasted_iota(jnp.int32, (1, slots), 1) < count_ref[0, 0]).astype(jnp.float32)

    expected = functools.reduce(
        lambda a, b: a + b, [present.astype(jnp.int32) for present, _ in greeted]
    )

    def remote(src, dst, send, recv, device):
        return pltpu.make_async_remote_copy(
            src_ref=src, dst_ref=dst, send_sem=send, recv_sem=recv, device_id=device, device_id_type=MESH
        )

    def piece(c):
        return pl.ds(c * rows, rows)

    def s_copy(t, way, c):
        src = found.at[t, MIRROR, piece(c)] if way == OTHER else state.at[t, piece(c)]
        device = [mirror, relay_to, (i, j + 1), (i, j - 1)][way]
        return remote(src, found.at[t, way, piece(c)], s_send.at[t, way, c], s_recv.at[t, way, c], device)

    s_goes = [has_mirror, can_relay, has_zp, has_zm]
    s_comes = [has_mirror, has_other, has_zm, has_zp]

    def send_state(t, c):
        for way in (MIRROR, BEFORE, AFTER):
            pl.when(s_goes[way])(s_copy(t, way, c).start)

    def relay(t, c):
        pl.when(has_mirror)(s_copy(t, MIRROR, c).wait_recv)
        pl.when(can_relay)(s_copy(t, OTHER, c).start)

    def p_at(t):
        return p_ref if t == 0 else p_mid.at[t - 1]

    corner_of = {(-1, -1): 0, (-1, 1): 1, (1, -1): 2, (1, 1): 3}

    def p_copies(t):
        copies = []
        for k, ((dx, dz), (present, device)) in enumerate(near.items()):
            if dz == 0:
                src = p_at(t).at[cx - 1 if dx > 0 else 0]
                dst = halo_x.at[t, 0 if dx > 0 else 1]
            elif dx == 0:
                src = face_z.at[t, 1 if dz > 0 else 0]
                dst = halo_z.at[t, 0 if dz > 0 else 1]
            else:
                src = face_c.at[t, corner_of[dx, dz]]
                dst = halo_c.at[t, corner_of[-dx, -dz]]
            copies.append(
                (present, near[-dx, -dz][0], remote(src, dst, p_send.at[t, k], p_recv.at[t, k], device))
            )
        return copies

    def stage_faces(t):
        for x in range(cx):
            face_z[t, 0, x : x + 1, :] = p_at(t)[x, 0:1, :]
            face_z[t, 1, x : x + 1, :] = p_at(t)[x, cz - 1 : cz, :]
        for (dx, dz), k in corner_of.items():
            face_c[t, k] = p_at(t)[cx - 1 if dx > 0 else 0, (cz - 1 if dz > 0 else 0) :][0:1, :]

    def send_faces(t):
        stage_faces(t)
        for goes, _, copy in p_copies(t):
            pl.when(goes)(copy.start)

    for way, present in enumerate(s_comes):

        @pl.when(jnp.logical_not(present))
        def _():
            for t in range(STEPS):
                found[t, way] = jnp.zeros((filt, slots), jnp.float32)

    for (dx, dz), (present, _) in near.items():

        @pl.when(jnp.logical_not(present))
        def _():
            for t in range(STEPS):
                if dz == 0:
                    halo_x[t, 0 if dx < 0 else 1] = jnp.zeros((cz, ny), jnp.float32)
                elif dx == 0:
                    halo_z[t, 0 if dz < 0 else 1] = jnp.zeros((cx, ny), jnp.float32)
                else:
                    halo_c[t, corner_of[dx, dz]] = jnp.zeros((1, ny), jnp.float32)

    pl.semaphore_wait(barrier, expected)
    for c in range(CHUNKS):
        send_state(0, c)
    send_faces(0)

    way_code = [0, 2 - upper, 1 + upper, 3, 4]
    slot_down = lax.broadcasted_iota(jnp.int32, (slots, slots), 0)
    for d, code in enumerate(way_code):
        gather[d] = (slot_down + code * slots == partner_ref[...]).astype(jnp.float32).astype(jnp.bfloat16)
    kind = [(material_ref[...] == m).astype(jnp.float32) for m in range(kinds)]
    in_t = jnp.transpose(jnp.concatenate([input_ref[...], output_ref[...]], axis=0))
    drive[...] = functools.reduce(lambda a, b: a + b, [in_t[:, m : m + 1] * kind[m] for m in range(kinds)])
    readout[...] = functools.reduce(
        lambda a, b: a + b, [in_t[:, kinds + m : kinds + m + 1] * kind[m] for m in range(kinds)]
    )
    for m in range(kinds):
        high, low = split(jnp.transpose(transition_ref[m]))
        here = slice(m * filt, (m + 1) * filt)
        mix_a[here, 0:filt] = high
        mix_a[here, filt : 2 * filt] = high
        mix_b[here, :] = low
    along = lax.rem(cell_ref[...], ny).astype(jnp.float32)
    place = jnp.transpose(jnp.broadcast_to(along, (lanes, slots)))
    lane = lax.broadcasted_iota(jnp.int32, (cz, lanes), 1).astype(jnp.float32)
    for x in range(cx):
        for part in range(ny // lanes):
            mask[x, :, part * lanes : (part + 1) * lanes] = (
                place[x * cz : (x + 1) * cz] == lane + float(part * lanes)
            ).astype(jnp.float32)

    def pick(x, change):
        chosen = mask[x] * change
        picked[pl.ds(x * cz, cz), :] = functools.reduce(
            lambda a, b: a + b, [chosen[:, k * lanes : (k + 1) * lanes] for k in range(ny // lanes)]
        )

    def picked_row():
        return jnp.sum(jnp.transpose(picked[...]), axis=0, keepdims=True)

    def first_change(x, _):
        pick(x, p_ref[x] - q_ref[x])
        return 0

    lax.fori_loop(0, cx, first_change, 0)
    velocity = picked_row()

    iota_z = lax.broadcasted_iota(jnp.int32, (cz, ny), 0)
    iota_y = lax.broadcasted_iota(jnp.int32, (cz, ny), 1)
    rest_w = face_w - edge_w

    def both_y(value):
        return jnp.where(iota_y == 0, 0.0, pltpu.roll(value, 1, 1)) + jnp.where(
            iota_y == ny - 1, 0.0, pltpu.roll(value, ny - 1, 1)
        )

    def plane(here, low, high):
        both_z = jnp.where(iota_z == 0, low, pltpu.roll(here, 1, 0)) + jnp.where(
            iota_z == cz - 1, high, pltpu.roll(here, cz - 1, 0)
        )
        line = edge_w * (here + both_z)
        side = line + both_y(line) + rest_w * here
        return line, both_z, side

    def pressure_free(t):
        for _, comes, copy in p_copies(t):
            pl.when(comes)(copy.wait_recv)
        now, before = p_at(t), (q_ref if t == 0 else p_at(t - 1))
        for end in (0, 1):
            low, high = halo_c[t, corner_of[2 * end - 1, -1]], halo_c[t, corner_of[2 * end - 1, 1]]
            beside[0 if end == 0 else cx + 1] = plane(halo_x[t, end], low, high)[2]

        def inner(x, _):
            here = now[x]
            low, high = halo_z[t, 0, pl.ds(x, 1), :], halo_z[t, 1, pl.ds(x, 1), :]
            line, both_z, side = plane(here, low, high)
            beside[x + 1] = side
            own = (
                line
                + both_y(line + rest_w * here)
                + rest_w * both_z
                + (centre_w - edge_w) * here
            )
            free[x] = 2.0 * here - before[x] + courant * own
            return 0

        lax.fori_loop(0, cx, inner, 0)

        def finish(x, _):
            value = free[x] + courant * (beside[x] + beside[x + 2])
            free[x] = value
            pick(x, value - now[x])
            return 0

        lax.fori_loop(0, cx, finish, 0)
        return picked_row()

    for t in range(STEPS):
        now = state[t]
        high, low = split(now)
        stacked = jnp.concatenate([high, low], axis=0)
        moved = dot(mix_a[...], stacked) + dot(mix_b[...], high)
        base = functools.reduce(
            lambda a, b: a + b, [moved[m * filt : (m + 1) * filt] * kind[m] for m in range(kinds)]
        )
        own = dot(stacked, gather[0])
        base = base + velocity * drive[...] + coupling * (own[:filt] + own[filt:] - now)
        relay(t, 0)
        for c in range(CHUNKS):
            if c + 1 < CHUNKS:
                relay(t, c + 1)
            total = base[c * rows : (c + 1) * rows]
            for way in (MIRROR, BEFORE, AFTER, OTHER):
                if way != MIRROR:
                    pl.when(s_comes[way])(s_copy(t, way, c).wait_recv)
                high, low = split(found[t, way, piece(c)])
                got = dot(jnp.concatenate([high, low], axis=0), gather[way + 1])
                total = total + coupling * (got[:rows] + got[rows:])
            state[t + 1, piece(c)] = total * live
            if t + 1 < STEPS:
                send_state(t + 1, c)
        change = pressure_free(t)
        product = state[t + 1] * readout[...]
        correction = jnp.sum(product, axis=0, keepdims=True)
        velocity = change - correction
        column = jnp.sum(jnp.transpose(product), axis=1, keepdims=True)
        for x in range(cx):
            value = free[x] - column[x * cz : (x + 1) * cz] * mask[x]
            if t + 1 < STEPS:
                p_mid[t, x] = value
            else:
                p_out[x] = value
        if t + 1 < STEPS:
            send_faces(t + 1)
    s_out[...] = jnp.transpose(state[STEPS])

    for t in range(STEPS):
        for way, goes in enumerate(s_goes):

            @pl.when(goes)
            def _():
                for c in range(CHUNKS):
                    s_copy(t, way, c).wait_send()

        for goes, _, copy in p_copies(t):
            pl.when(goes)(copy.wait_send)


def per_device(
    pressure,
    previous,
    states,
    wall_cell,
    wall_count,
    material,
    partner,
    transitions,
    inputs,
    outputs,
):
    cx, cz, ny = pressure.shape
    slots, filt = states.shape[2:]
    kinds = transitions.shape[0]
    sizes = (lax.axis_size("gx"), lax.axis_size("gz"))
    f32, bf16 = jnp.float32, jnp.bfloat16
    vmem = pl.BlockSpec(memory_space=pltpu.VMEM)
    smem = pl.BlockSpec(memory_space=pltpu.SMEM)
    pressure_out, states_out = pl.pallas_call(
        functools.partial(kernel, sizes),
        out_shape=[
            jax.ShapeDtypeStruct((cx, cz, ny), f32),
            jax.ShapeDtypeStruct((slots, filt), f32),
        ],
        in_specs=[vmem, vmem, vmem, vmem, smem, vmem, vmem, vmem, vmem, vmem],
        out_specs=[vmem, vmem],
        scratch_shapes=[
            pltpu.VMEM((STEPS + 1, filt, slots), f32),
            pltpu.VMEM((STEPS, 4, filt, slots), f32),
            pltpu.VMEM((5, slots, slots), bf16),
            pltpu.VMEM((kinds * filt, 2 * filt), bf16),
            pltpu.VMEM((kinds * filt, filt), bf16),
            pltpu.VMEM((filt, slots), f32),
            pltpu.VMEM((filt, slots), f32),
            pltpu.VMEM((cx, cz, ny), f32),
            pltpu.VMEM((STEPS - 1, cx, cz, ny), f32),
            pltpu.VMEM((STEPS, 2, cz, ny), f32),
            pltpu.VMEM((STEPS, 2, cx, ny), f32),
            pltpu.VMEM((STEPS, 4, 1, ny), f32),
            pltpu.VMEM((STEPS, 2, cx, ny), f32),
            pltpu.VMEM((STEPS, 4, 1, ny), f32),
            pltpu.VMEM((cx + 2, cz, ny), f32),
            pltpu.VMEM((cx, cz, ny), f32),
            pltpu.VMEM((slots, 128), f32),
            pltpu.SemaphoreType.DMA((STEPS, 4, CHUNKS)),
            pltpu.SemaphoreType.DMA((STEPS, 4, CHUNKS)),
            pltpu.SemaphoreType.DMA((STEPS, 8)),
            pltpu.SemaphoreType.DMA((STEPS, 8)),
        ],
        compiler_params=pltpu.CompilerParams(
            collective_id=0, has_side_effects=True, vmem_limit_bytes=40 * 1024 * 1024
        ),
        name="leapfrog",
    )(
        pressure,
        previous,
        states.reshape(slots, filt),
        wall_cell.reshape(1, slots),
        wall_count,
        material.reshape(1, slots),
        partner.reshape(1, slots),
        transitions,
        inputs,
        outputs,
    )
    return pressure_out, states_out.reshape(1, 1, slots, filt)


def solution(mesh):
    placed = (
        P("gx", "gz", None),
        P("gx", "gz", None),
        P("gx", "gz", None, None),
        P("gx", "gz", None),
        P("gx", "gz"),
        P("gx", "gz", None),
        P("gx", "gz", None),
        P(),
        P(),
        P(),
    )
    return jax.shard_map(
        per_device,
        mesh=mesh,
        in_specs=placed,
        out_specs=(P("gx", "gz", None), P("gx", "gz", None, None)),
        check_vma=False,
    )
```

time: 202 us -> 63.5 us (0.31)
  the two profiles are of different devices: /device:TPU:30 before, /device:TPU:5 now
where the time goes in v1:
time: 63.5 us; the launch traced here: 63.2 us
  Pallas kernels  55.8 us (88%)
  local copies, waits for them, and re-layouts  6.09 us (10%)
  between operations  1.33 us (2%)
    pallas_call x1, Pallas kernels, per_device(): pl.pallas_call(functools.partial(kernel, sizes), out_shape=[jax.ShapeDtyp...  55.8 us
    unnamed x20, local copies, waits for them, and re-layouts  6.09 us

profile of v1, /device:TPU:5, one launch (start us, length us, event | category | flops | bytes accessed | tf_op | source)
XLA Modules:
  0.0 63.2 jit_solution(5593063769168234546)
XLA Ops:
  1.3 0.0 copy-start.7
  1.3 0.0 copy-start.8
  1.3 0.0 copy-start.5
  1.3 0.0 copy-start.4
  1.3 0.0 copy-start.6
  1.3 0.6 copy-done.7
  2.0 0.0 copy-done.8
  2.0 0.0 copy-done.5
  2.0 0.0 copy-done.4
  2.0 0.0 copy-done.6
  2.0 0.0 copy-start
  2.0 1.0 %copy-done = f32[16,16,512]{2,1,0:T(8,128)S(1)} copy-done((f32[16,16,512]{2,1,0:T(8,128)S(1)}, f32[16,16,512]{2,1,0:T(8,128)}, u32[]{:S(2)}) %copy-start) | copy-done | bytes 524312
  3.1 0.0 copy-start.1
  3.1 1.0 %copy-done.1 = f32[16,16,512]{2,1,0:T(8,128)S(1)} copy-done((f32[16,16,512]{2,1,0:T(8,128)S(1)}, f32[16,16,512]{2,1,0:T(8,128)}, u32[]{:S(2)}) %copy-start.1) | copy-done | bytes 524312
  4.1 0.0 copy-start.2
  4.1 0.9 %copy-done.2 = f32[4,128,128]{2,1,0:T(8,128)S(1)} copy-done((f32[4,128,128]{2,1,0:T(8,128)S(1)}, f32[4,128,128]{2,1,0:T(8,128)}, u32[]{:S(2)}) %copy-start.2) | copy-done | bytes 262168
  5.1 0.0 copy-start.3
  5.1 0.9 %copy-done.3 = f32[1,1,256,128]{3,2,1,0:T(8,128)S(1)} copy-done((f32[1,1,256,128]{3,2,1,0:T(8,128)S(1)}, f32[1,1,256,128]{3,2,1,0:T(8,128)}, u32[]{:S(2)}) %copy-start.3) | copy-done | bytes 131096
  6.0 55.8 %leapfrog.1 = (f32[16,16,512]{2,1,0:T(8,128)S(1)}, f32[256,128]{1,0:T(8,128)S(1)}) custom-call(f32[16,16,512]{2,1,0:T(8,128)S(1)} %copy-done, f32[16,16,512]{2,1,0:T(8,128)S(1)} %copy-done.1, f32[256,128]{1,0:T(8,128)S(1)} %bitcast.5, s32[1,256]{1,0:T(1,128)S(1)} %bitcast.7, s32[1,1]{1,0:T(1,128)S(6)} %copy.14.count_ref, s32[1,256]{1,0:T(1,128)S(1)} %bitcast.8, ...), custom_call_target="tpu_custom_call" | custom-call | tf_op jit(solution)/shard_map/leapfrog/pallas_call | solution.py:356
  61.8 0.8 %copy.15 = f32[16,16,512]{2,1,0:T(8,128)} copy(f32[16,16,512]{2,1,0:T(8,128)S(1)} %get-tuple-element.8) | data formatting | bytes 1048576
  62.5 0.7 %copy.16 = f32[1,1,256,128]{3,2,1,0:T(8,128)} copy(f32[1,1,256,128]{3,2,1,0:T(8,128)S(1)} %bitcast.6) | data formatting | bytes 262144
Async XLA Ops:
  1.3 0.7 %copy-start.7 = (s32[1,1,256]{2,1,0:T(1,128)S(1)}, s32[1,1,256]{2,1,0:T(1,128)}, u32[]{:S(2)}) copy-start(s32[1,1,256]{2,1,0:T(1,128)} %param.15) | copy-start | bytes 3076
  1.3 0.7 %copy-start.8 = (s32[1,1,256]{2,1,0:T(1,128)S(1)}, s32[1,1,256]{2,1,0:T(1,128)}, u32[]{:S(2)}) copy-start(s32[1,1,256]{2,1,0:T(1,128)} %param.16) | copy-start | bytes 3076
  1.3 0.7 %copy-start.5 = (f32[4,128]{1,0:T(4,128)S(1)}, f32[4,128]{1,0:T(4,128)}, u32[]{:S(2)}) copy-start(f32[4,128]{1,0:T(4,128)} %output_ref.1) | copy-start | bytes 6148
  1.3 0.7 %copy-start.4 = (f32[4,128]{1,0:T(4,128)S(1)}, f32[4,128]{1,0:T(4,128)}, u32[]{:S(2)}) copy-start(f32[4,128]{1,0:T(4,128)} %input_ref.1) | copy-start | bytes 6148
  1.3 0.7 %copy-start.6 = (s32[1,1,256]{2,1,0:T(1,128)S(1)}, s32[1,1,256]{2,1,0:T(1,128)}, u32[]{:S(2)}) copy-start(s32[1,1,256]{2,1,0:T(1,128)} %param.13) | copy-start | bytes 3076
  2.0 1.0 %copy-start = (f32[16,16,512]{2,1,0:T(8,128)S(1)}, f32[16,16,512]{2,1,0:T(8,128)}, u32[]{:S(2)}) copy-start(f32[16,16,512]{2,1,0:T(8,128)} %p_ref.1) | copy-start | bytes 1572868
  3.1 1.0 %copy-start.1 = (f32[16,16,512]{2,1,0:T(8,128)S(1)}, f32[16,16,512]{2,1,0:T(8,128)}, u32[]{:S(2)}) copy-start(f32[16,16,512]{2,1,0:T(8,128)} %q_ref.1) | copy-start | bytes 1572868
  4.1 0.9 %copy-start.2 = (f32[4,128,128]{2,1,0:T(8,128)S(1)}, f32[4,128,128]{2,1,0:T(8,128)}, u32[]{:S(2)}) copy-start(f32[4,128,128]{2,1,0:T(8,128)} %transition_ref.1) | copy-start | bytes 786436
  5.1 0.9 %copy-start.3 = (f32[1,1,256,128]{3,2,1,0:T(8,128)S(1)}, f32[1,1,256,128]{3,2,1,0:T(8,128)}, u32[]{:S(2)}) copy-start(f32[1,1,256,128]{3,2,1,0:T(8,128)} %param.12) | copy-start | bytes 393220

commit v2 on v1

v2 whole, which is shorter than its diff:
```python
import functools

import jax
import jax.numpy as jnp
from jax import lax
from jax.experimental import pallas as pl
from jax.experimental.pallas import tpu as pltpu
from jax.sharding import PartitionSpec as P

MESH = pl.DeviceIdType.MESH
STEPS = 3
CHUNKS = 2
PRESSURE_AT = (0, 1, 1)
SEND_ORDER = 2
OTHER, BEFORE, AFTER = range(3)
OWN, MIRROR = range(2)

face_w = 0.5
edge_w = 0.0625
corner_w = 0.0625
centre_w = -(6 * face_w + 12 * edge_w + 8 * corner_w)
courant = 0.3
coupling = 0.3


def split(value):
    high = value.astype(jnp.bfloat16)
    low = (value - high.astype(jnp.float32)).astype(jnp.bfloat16)
    return high, low


def dot(left, right):
    return jnp.dot(left, right, preferred_element_type=jnp.float32)


def kernel(
    sizes,
    p_hbm,
    q_hbm,
    s_hbm,
    cell_hbm,
    count_ref,
    material_hbm,
    partner_hbm,
    transition_hbm,
    input_hbm,
    output_hbm,
    p_out,
    s_out,
    q_ref,
    s_ref,
    cell_ref,
    material_ref,
    partner_ref,
    transition_ref,
    input_ref,
    output_ref,
    state,
    found,
    base,
    info_out,
    info_in,
    v_out,
    v_in,
    kind,
    gather,
    mix_a,
    mix_b,
    drive,
    readout,
    mask,
    pressure,
    halo_z,
    halo_c,
    face_z,
    face_c,
    edge_out,
    edge_in,
    turned,
    column,
    free,
    picked,
    load_sem,
    store_sem,
    info_sem,
    x_send,
    x_recv,
    v_send,
    v_recv,
    s_send,
    s_recv,
    p_send,
    p_recv,
    e_send,
    e_recv,
):
    n_gx, n_gz = sizes
    cx, cz, ny = q_ref.shape
    slots, filt = s_ref.shape
    kinds = transition_ref.shape[0]
    rows = filt // CHUNKS
    lanes = 128
    parts = ny // lanes
    i, j = lax.axis_index("gx"), lax.axis_index("gz")
    upper = lax.rem(i, 2)
    has_xm, has_xp = i > 0, i < n_gx - 1
    has_zm, has_zp = j > 0, j < n_gz - 1
    mirror = (i + 1 - 2 * upper, j)
    up_to, down_to = (i + 2 - 4 * upper, j), (i - 2 + 4 * upper, j)
    has_up = jnp.logical_and(up_to[0] >= 0, up_to[0] < n_gx)
    has_down = jnp.logical_and(down_to[0] >= 0, down_to[0] < n_gx)

    near = {}
    for dx in (-1, 0, 1):
        for dz in (-1, 0, 1):
            if dx or dz:
                present = [has_xm, None, has_xp][dx + 1], [has_zm, None, has_zp][dz + 1]
                present = [one for one in present if one is not None]
                near[dx, dz] = (functools.reduce(jnp.logical_and, present), (i + dx, j + dz))
    order = {way: k for k, way in enumerate(near)}
    corner_of = {(-1, -1): 0, (-1, 1): 1, (1, -1): 2, (1, 1): 3}
    greeted = list(near.values()) + [(i >= 2, (i - 2, j)), (i < n_gx - 2, (i + 2, j))]

    barrier = pltpu.get_barrier_semaphore()
    for present, device in greeted:

        @pl.when(present)
        def _():
            pl.semaphore_signal(barrier, inc=1, device_id=device, device_id_type=MESH)

    expected = functools.reduce(
        lambda a, b: a + b, [present.astype(jnp.int32) for present, _ in greeted]
    )

    stores = [
        pltpu.make_async_copy(src, dst, store_sem.at[k])
        for k, (src, dst) in enumerate(
            [
                (s_ref, s_out),
                (free.at[STEPS - 1, 1 : cx - 1], p_out.at[1 : cx - 1]),
                (free.at[STEPS - 1, 0], p_out.at[0]),
                (free.at[STEPS - 1, cx - 1], p_out.at[cx - 1]),
            ]
        )
    ]
    loads = [
        pltpu.make_async_copy(src, dst, load_sem.at[k])
        for k, (src, dst) in enumerate(
            [
                (s_hbm, s_ref),
                (p_hbm, pressure.at[0, 1 : cx + 1]),
                (q_hbm, q_ref),
                (cell_hbm, cell_ref),
                (partner_hbm, partner_ref),
                (material_hbm, material_ref),
                (input_hbm, input_ref),
                (output_hbm, output_ref),
                (transition_hbm, transition_ref),
            ]
        )
    ]
    for load in loads:
        load.start()

    def remote(src, dst, send, recv, device):
        return pltpu.make_async_remote_copy(
            src_ref=src, dst_ref=dst, send_sem=send, recv_sem=recv, device_id=device, device_id_type=MESH
        )

    def piece(c):
        return pl.ds(c * rows, rows)

    def sides(t):
        return (OWN, MIRROR) if t + 1 < STEPS else (OWN,)

    def cross(c):
        return remote(state.at[OWN, 0, piece(c)], state.at[MIRROR, 0, piece(c)], x_send.at[c], x_recv.at[c], mirror)

    s_goes = [[has_up, has_zp, has_zm], [has_down, has_zp, has_zm]]
    s_comes = [[has_down, has_zm, has_zp], [has_up, has_zm, has_zp]]

    def s_copy(t, side, way, c):
        source = 1 - side if way == OTHER else side
        device = [down_to if side else up_to, (i, j + 1), (i, j - 1)][way]
        return remote(
            state.at[source, t, piece(c)],
            found.at[t, side, way, piece(c)],
            s_send.at[t, side, way, c],
            s_recv.at[t, side, way, c],
            device,
        )

    def send_state(t, source, c):
        for side in sides(t):
            for way in (OTHER, BEFORE, AFTER):
                if (1 - side if way == OTHER else side) == source:
                    pl.when(s_goes[side][way])(s_copy(t, side, way, c).start)

    def v_copy(t):
        return remote(v_out.at[t], v_in.at[t], v_send.at[t], v_recv.at[t], mirror)

    about = remote(info_out, info_in, info_sem.at[0], info_sem.at[1], mirror)

    def plane_at(t, x):
        return pressure.at[0, x + 1] if t == 0 else free.at[t - 1, x]

    def p_copies(t):
        copies = []
        for (dx, dz), (present, device) in near.items():
            k = order[dx, dz]
            if dz == 0:
                src = plane_at(t, cx - 1 if dx > 0 else 0)
                dst = pressure.at[t, 0 if dx > 0 else cx + 1]
            elif dx == 0:
                src = face_z.at[t, 1 if dz > 0 else 0]
                dst = halo_z.at[t, 0 if dz > 0 else 1]
            else:
                src = face_c.at[t, corner_of[dx, dz]]
                dst = halo_c.at[t, corner_of[-dx, -dz]]
            copies.append(
                (present, near[-dx, -dz][0], remote(src, dst, p_send.at[t, k], p_recv.at[t, k], device))
            )
        return copies

    def send_faces(t):
        for x in range(cx):
            here = plane_at(t, x)
            face_z[t, 0, x : x + 1, :] = here[0:1, :]
            face_z[t, 1, x : x + 1, :] = here[cz - 1 : cz, :]
        for (dx, dz), k in corner_of.items():
            here = plane_at(t, cx - 1 if dx > 0 else 0)
            z = cz - 1 if dz > 0 else 0
            face_c[t, k] = here[z : z + 1, :]
        for goes, _, copy in p_copies(t):
            pl.when(goes)(copy.start)

    def e_copies(t):
        copies = []
        for (dx, dz), (present, device) in near.items():
            k = order[dx, dz]
            copy = remote(
                edge_out.at[t],
                edge_in.at[t, order[-dx, -dz]],
                e_send.at[t, k],
                e_recv.at[t, k],
                device,
            )
            copies.append((present, near[-dx, -dz][0], copy))
        return copies

    def send_edges(t, row):
        edge_out[t] = row
        for goes, _, copy in e_copies(t):
            pl.when(goes)(copy.start)

    for side in (OWN, MIRROR):
        for way, present in enumerate(s_comes[side]):

            @pl.when(jnp.logical_not(present))
            def _():
                for t in range(STEPS - side):
                    found[t, side, way] = jnp.zeros((filt, slots), jnp.float32)

    for (dx, dz), (present, _) in near.items():

        @pl.when(jnp.logical_not(present))
        def _():
            for t in range(STEPS):
                edge_in[t, order[dx, dz]] = jnp.zeros((1, slots), jnp.float32)
                if dz == 0:
                    pressure[t, 0 if dx < 0 else cx + 1] = jnp.zeros((cz, ny), jnp.float32)
                elif dx == 0:
                    halo_z[t, 0 if dz < 0 else 1] = jnp.zeros((cx, ny), jnp.float32)
                else:
                    halo_c[t, corner_of[dx, dz]] = jnp.zeros((1, ny), jnp.float32)

    live = (lax.broadcasted_iota(jnp.int32, (1, slots), 1) < count_ref[0, 0]).astype(jnp.float32)
    loads[0].wait()
    state[OWN, 0] = jnp.transpose(s_ref[...]) * live
    pl.semaphore_wait(barrier, expected)
    def send_own():
        for c in range(CHUNKS):
            send_state(0, OWN, c)

    if SEND_ORDER == 2:
        loads[1].wait()
        send_faces(0)
    for c in range(CHUNKS):
        cross(c).start()
    if SEND_ORDER == 0:
        send_own()
    if SEND_ORDER <= 1:
        loads[1].wait()
        send_faces(0)
    if SEND_ORDER == 1:
        send_own()
    for k, load in enumerate(loads):
        if k > 1:
            load.wait()
    info_out[...] = jnp.concatenate(
        [
            partner_ref[...].astype(jnp.float32),
            material_ref[...].astype(jnp.float32),
            live,
            jnp.zeros((5, slots), jnp.float32),
        ],
        axis=0,
    )
    about.start()

    along = lax.rem(cell_ref[...], ny).astype(jnp.float32)
    column[...] = jnp.transpose(jnp.broadcast_to(along, (lanes, slots)))
    send_edges(0, along)
    lane = lax.broadcasted_iota(jnp.int32, (cz, lanes), 1).astype(jnp.float32)
    for x in range(cx):
        for part in range(parts):
            mask[x, :, part * lanes : (part + 1) * lanes] = (
                column[x * cz : (x + 1) * cz] == lane + float(part * lanes)
            ).astype(jnp.float32)

    in_t = jnp.transpose(jnp.concatenate([input_ref[...], output_ref[...]], axis=0))
    slot_down = lax.broadcasted_iota(jnp.int32, (slots, slots), 0).astype(jnp.float32)

    def describe(side, partner, material):
        low_x, high_x = 1.0, 2.0
        is_upper = (upper if side == OWN else 1 - upper).astype(jnp.float32)
        for d, code in enumerate([0.0, high_x - is_upper, low_x + is_upper, 3.0, 4.0]):
            gather[side, d] = (slot_down + code * slots == partner).astype(jnp.float32).astype(jnp.bfloat16)
        for m in range(kinds):
            kind[side, m] = (material == float(m)).astype(jnp.float32)
        for target, first in ((drive, 0), (readout, kinds)):
            target[side] = functools.reduce(
                lambda a, b: a + b, [in_t[:, first + m : first + m + 1] * kind[side, m] for m in range(kinds)]
            )

    describe(OWN, partner_ref[...].astype(jnp.float32), material_ref[...].astype(jnp.float32))
    for m in range(kinds):
        high, low = split(jnp.transpose(transition_ref[m]))
        here = slice(m * filt, (m + 1) * filt)
        mix_a[here, 0:filt] = high
        mix_a[here, filt : 2 * filt] = high
        mix_b[here, :] = low

    def pick(x, change):
        chosen = mask[x] * change
        picked[pl.ds(x * cz, cz), :] = functools.reduce(
            lambda a, b: a + b, [chosen[:, k * lanes : (k + 1) * lanes] for k in range(parts)]
        )

    def picked_row():
        return jnp.sum(jnp.transpose(picked[...]), axis=0, keepdims=True)

    def first_change(x, _):
        pick(x, pressure[0, x + 1] - q_ref[x])
        return 0

    lax.fori_loop(0, cx, first_change, 0, unroll=4)
    velocity = [picked_row(), None]
    v_out[0] = velocity[OWN]
    v_copy(0).start()

    iota_z = lax.broadcasted_iota(jnp.int32, (cz, ny), 0)
    iota_y = lax.broadcasted_iota(jnp.int32, (cz, ny), 1)
    rest_w = face_w - edge_w

    def both_y(value):
        return jnp.where(iota_y == 0, 0.0, pltpu.roll(value, 1, 1)) + jnp.where(
            iota_y == ny - 1, 0.0, pltpu.roll(value, ny - 1, 1)
        )

    def both_z(here, low, high):
        return jnp.where(iota_z == 0, low, pltpu.roll(here, 1, 0)) + jnp.where(
            iota_z == cz - 1, high, pltpu.roll(here, cz - 1, 0)
        )

    def turn_edges(t, slot, ways):
        none = jnp.zeros((1, slots), jnp.float32)
        rows_in = [edge_in[t, k] if way in ways else none for way, k in order.items()]
        turned[slot, :, 0:8] = jnp.transpose(jnp.concatenate(rows_in, axis=0))

    def spread(way):
        (dx, dz), k = way, order[way]
        x, z = (0 if dx > 0 else cx - 1), (0 if dz > 0 else cz - 1)
        if dz == 0:
            at = pl.ds(x * cz, cz)
        elif dx == 0:
            at = pl.ds(z, cx, cz)
        else:
            at = pl.ds(x * cz + z, 1)
        place, value = turned[0, at, :][:, k : k + 1], turned[2 if dx else 1, at, :][:, k : k + 1]
        along_y = lax.broadcasted_iota(jnp.int32, (place.shape[0], ny), 1).astype(jnp.float32)
        return jnp.where(place == along_y, value, 0.0)

    along_z = [way for way in order if way[0] == 0]
    along_x = [way for way in order if way[0] != 0]

    def wait_for(t, ways):
        copies = p_copies(t)
        if t > 0:
            copies += e_copies(t)
        for n, (_, comes, copy) in enumerate(copies):
            if list(order)[n % 8] in ways:
                pl.when(comes)(copy.wait_recv)

    def pressure_free(t):
        last = t + 1 == STEPS

        def inside(x):
            return both_z(pressure[t, x + 1], halo_z[t, 0, pl.ds(x, 1), :], halo_z[t, 1, pl.ds(x, 1), :])

        def one(x, before, here, after):
            left, mid, right = pressure[t, x], pressure[t, x + 1], pressure[t, x + 2]
            past = q_ref[x] if t == 0 else pressure[t - 1, x + 1]
            beside = left + right
            even = edge_w * ((beside + mid) + (before + here + after))
            total = both_y(even + rest_w * mid) + even + rest_w * (here + beside) + (centre_w - edge_w) * mid
            value = 2.0 * mid - past + courant * total
            if last:
                free[t, x] = value - column[pl.ds(x * cz, cz), 0:1] * mask[x]
            else:
                free[t, x] = value
                pick(x, value - mid)

        def step(x, held):
            before, here = held
            after = inside(x + 1)
            one(x, before, here, after)
            return here, after

        if t == 1:
            for _, comes, copy in e_copies(0):
                pl.when(comes)(copy.wait_recv)
            turn_edges(0, 0, list(order))
        wait_for(t, along_z)
        if t > 0:
            turn_edges(t, 1, along_z)
            for end in (0, 1):
                halo_z[t, end] -= spread((0, 2 * end - 1))
        before, here = lax.fori_loop(1, cx - 1, step, (inside(0), inside(1)), unroll=2)
        if last:
            stores[1].start()
        wait_for(t, along_x)
        if t > 0:
            turn_edges(t, 2, along_x)
            for end in (0, 1):
                side = 2 * end - 1
                pressure[t, end * (cx + 1)] -= spread((side, 0))
                for z in (-1, 1):
                    halo_c[t, corner_of[side, z]] -= spread((side, z))

        def ends(end):
            at = [halo_c[t, corner_of[2 * end - 1, z]] for z in (-1, 1)]
            return both_z(pressure[t, end * (cx + 1)], *at)

        one(cx - 1, before, here, ends(1))
        one(0, ends(0), inside(0), inside(1))
        if last:
            stores[2].start()
            stores[3].start()
            return None
        return picked_row()

    def gathered(side, d, value):
        high, low = split(value)
        got = dot(jnp.concatenate([high, low], axis=0), gather[side, d])
        return got[: value.shape[0]] + got[value.shape[0] :]

    def mixed(side, t):
        now = state[side, t]
        high, low = split(now)
        stacked = jnp.concatenate([high, low], axis=0)
        moved = dot(mix_a[...], stacked) + dot(mix_b[...], high)
        total = functools.reduce(
            lambda a, b: a + b, [moved[m * filt : (m + 1) * filt] * kind[side, m] for m in range(kinds)]
        )
        own = dot(stacked, gather[side, 0])
        base[side] = total + coupling * (own[:filt] + own[filt:] - now)

    def across(side, t):
        base[side] += velocity[side] * drive[side] + coupling * gathered(side, 1, state[1 - side, t])

    def do_pressure(t):
        change = pressure_free(t)
        if t + 1 == STEPS:
            return None
        if t + 2 < STEPS:
            v_out[t + 1] = change
            v_copy(t + 1).start()
        send_faces(t + 1)
        return change

    def come(side, t):
        for c in range(CHUNKS):
            total = base[side, piece(c)]
            for way in (OTHER, BEFORE, AFTER):
                pl.when(s_comes[side][way])(s_copy(t, side, way, c).wait_recv)
                total = total + coupling * gathered(side, way + 2, found[t, side, way, piece(c)])
            state[side, t + 1, piece(c)] = total * lives[side]
            if t + 1 < STEPS and (c + 1 < CHUNKS or side == MIRROR):
                send_state(t + 1, side, c)

    if SEND_ORDER == 2:
        send_own()
    mixed(OWN, 0)
    for c in range(CHUNKS):
        cross(c).wait_recv()
        send_state(0, MIRROR, c)
    about.wait_recv()
    describe(MIRROR, info_in[0:1, :], info_in[1:2, :])
    lives = [live, info_in[2:3, :]]

    for t in range(STEPS):
        if t > 0:
            mixed(OWN, t)
        across(OWN, t)
        if PRESSURE_AT[t] == 0:
            change = do_pressure(t)
        come(OWN, t)
        product = state[OWN, t + 1] * readout[OWN]
        if t + 1 < STEPS:
            correction = jnp.sum(product, axis=0, keepdims=True)
            send_edges(t + 1, correction)
            send_state(t + 1, OWN, CHUNKS - 1)
        else:
            s_ref[...] = jnp.transpose(state[OWN, STEPS])
            stores[0].start()
        column[...] = jnp.broadcast_to(jnp.sum(jnp.transpose(product), axis=1, keepdims=True), (slots, lanes))
        if PRESSURE_AT[t] == 1:
            change = do_pressure(t)
        if t + 1 < STEPS:
            mixed(MIRROR, t)
            v_copy(t).wait_recv()
            velocity[MIRROR] = v_in[t] - (behind if t > 0 else 0.0)
            across(MIRROR, t)
            come(MIRROR, t)
            behind = jnp.sum(state[MIRROR, t + 1] * readout[MIRROR], axis=0, keepdims=True)
            if PRESSURE_AT[t] == 2:
                change = do_pressure(t)
            velocity[OWN] = change - correction
            for x in range(cx):
                pressure[t + 1, x + 1] = free[t, x] - column[x * cz : (x + 1) * cz, 0:1] * mask[x]

    for store in stores:
        store.wait()
    about.wait_send()
    for c in range(CHUNKS):
        cross(c).wait_send()
    for t in range(STEPS - 1):
        v_copy(t).wait_send()
    for t in range(STEPS):
        for side in sides(t):
            for way, goes in enumerate(s_goes[side]):

                @pl.when(goes)
                def _():
                    for c in range(CHUNKS):
                        s_copy(t, side, way, c).wait_send()

        for goes, _, copy in p_copies(t) + e_copies(t):
            pl.when(goes)(copy.wait_send)


def hand_over(p_ref, s_ref, p_out, s_out, p_held, s_held, load_sem, store_sem):
    part = p_ref.shape[0] // 4
    pieces = [(s_ref, s_held, s_out)] + [
        (p_ref.at[here], p_held.at[here], p_out.at[here]) for here in [pl.ds(k * part, part) for k in range(4)]
    ]
    loads = [pltpu.make_async_copy(src, held, load_sem.at[k]) for k, (src, held, _) in enumerate(pieces)]
    stores = [pltpu.make_async_copy(held, dst, store_sem.at[k]) for k, (_, held, dst) in enumerate(pieces)]
    for load in loads:
        load.start()
    for load, store in zip(loads, stores):
        load.wait()
        store.start()
    for store in stores:
        store.wait()


def per_device(
    pressure,
    previous,
    states,
    wall_cell,
    wall_count,
    material,
    partner,
    transitions,
    inputs,
    outputs,
):
    cx, cz, ny = pressure.shape
    slots, filt = states.shape[2:]
    kinds = transitions.shape[0]
    sizes = (lax.axis_size("gx"), lax.axis_size("gz"))
    f32, bf16 = jnp.float32, jnp.bfloat16
    vmem = pl.BlockSpec(memory_space=pltpu.VMEM)
    smem = pl.BlockSpec(memory_space=pltpu.SMEM)
    hbm = pl.BlockSpec(memory_space=pltpu.HBM)
    pressure_out, states_out = pl.pallas_call(
        functools.partial(kernel, sizes),
        out_shape=[
            jax.ShapeDtypeStruct((cx, cz, ny), f32),
            jax.ShapeDtypeStruct((slots, filt), f32),
        ],
        in_specs=[hbm, hbm, hbm, hbm, smem, hbm, hbm, hbm, hbm, hbm],
        out_specs=[hbm, hbm],
        scratch_shapes=[
            pltpu.VMEM((cx, cz, ny), f32),
            pltpu.VMEM((slots, filt), f32),
            pltpu.VMEM((1, slots), jnp.int32),
            pltpu.VMEM((1, slots), jnp.int32),
            pltpu.VMEM((1, slots), jnp.int32),
            pltpu.VMEM((kinds, filt, filt), f32),
            pltpu.VMEM((kinds, filt), f32),
            pltpu.VMEM((kinds, filt), f32),
            pltpu.VMEM((2, STEPS + 1, filt, slots), f32),
            pltpu.VMEM((STEPS, 2, 3, filt, slots), f32),
            pltpu.VMEM((2, filt, slots), f32),
            pltpu.VMEM((8, slots), f32),
            pltpu.VMEM((8, slots), f32),
            pltpu.VMEM((STEPS - 1, 1, slots), f32),
            pltpu.VMEM((STEPS - 1, 1, slots), f32),
            pltpu.VMEM((2, kinds, 1, slots), f32),
            pltpu.VMEM((2, 5, slots, slots), bf16),
            pltpu.VMEM((kinds * filt, 2 * filt), bf16),
            pltpu.VMEM((kinds * filt, filt), bf16),
            pltpu.VMEM((2, filt, slots), f32),
            pltpu.VMEM((2, filt, slots), f32),
            pltpu.VMEM((cx, cz, ny), f32),
            pltpu.VMEM((STEPS, cx + 2, cz, ny), f32),
            pltpu.VMEM((STEPS, 2, cx, ny), f32),
            pltpu.VMEM((STEPS, 4, 1, ny), f32),
            pltpu.VMEM((STEPS, 2, cx, ny), f32),
            pltpu.VMEM((STEPS, 4, 1, ny), f32),
            pltpu.VMEM((STEPS, 1, slots), f32),
            pltpu.VMEM((STEPS, 8, 1, slots), f32),
            pltpu.VMEM((3, slots, 128), f32),
            pltpu.VMEM((slots, 128), f32),
            pltpu.VMEM((STEPS, cx, cz, ny), f32),
            pltpu.VMEM((slots, 128), f32),
            pltpu.SemaphoreType.DMA((9,)),
            pltpu.SemaphoreType.DMA((4,)),
            pltpu.SemaphoreType.DMA((2,)),
            pltpu.SemaphoreType.DMA((CHUNKS,)),
            pltpu.SemaphoreType.DMA((CHUNKS,)),
            pltpu.SemaphoreType.DMA((STEPS - 1,)),
            pltpu.SemaphoreType.DMA((STEPS - 1,)),
            pltpu.SemaphoreType.DMA((STEPS, 2, 3, CHUNKS)),
            pltpu.SemaphoreType.DMA((STEPS, 2, 3, CHUNKS)),
            pltpu.SemaphoreType.DMA((STEPS, 8)),
            pltpu.SemaphoreType.DMA((STEPS, 8)),
            pltpu.SemaphoreType.DMA((STEPS, 8)),
            pltpu.SemaphoreType.DMA((STEPS, 8)),
        ],
        compiler_params=pltpu.CompilerParams(
            collective_id=0, has_side_effects=True, vmem_limit_bytes=60 * 1024 * 1024
        ),
        name="leapfrog",
    )(
        pressure,
        previous,
        states.reshape(slots, filt),
        wall_cell.reshape(1, slots),
        wall_count,
        material.reshape(1, slots),
        partner.reshape(1, slots),
        transitions,
        inputs,
        outputs,
    )
    pressure_out, states_out = pl.pallas_call(
        hand_over,
        out_shape=[
            jax.ShapeDtypeStruct((cx, cz, ny), f32),
            jax.ShapeDtypeStruct((slots, filt), f32),
        ],
        in_specs=[hbm, hbm],
        out_specs=[hbm, hbm],
        scratch_shapes=[
            pltpu.VMEM((cx, cz, ny), f32),
            pltpu.VMEM((slots, filt), f32),
            pltpu.SemaphoreType.DMA((5,)),
            pltpu.SemaphoreType.DMA((5,)),
        ],
        name="hand_over",
    )(pressure_out, states_out)
    return pressure_out, states_out.reshape(1, 1, slots, filt)


def solution(mesh):
    placed = (
        P("gx", "gz", None),
        P("gx", "gz", None),
        P("gx", "gz", None, None),
        P("gx", "gz", None),
        P("gx", "gz"),
        P("gx", "gz", None),
        P("gx", "gz", None),
        P(),
        P(),
        P(),
    )
    return jax.shard_map(
        per_device,
        mesh=mesh,
        in_specs=placed,
        out_specs=(P("gx", "gz", None), P("gx", "gz", None, None)),
        check_vma=False,
    )
```

time: 63.5 us -> 52.7 us (0.83)
  the two profiles are of different devices: /device:TPU:5 before, /device:TPU:57 now
where the time goes in v2:
time: 52.7 us; the launch traced here: 52.6 us
  Pallas kernels  51.3 us (97%)
  between operations  1.29 us (2%)
    pallas_call x1, Pallas kernels, per_device(): pl.pallas_call(functools.partial(kernel, sizes), out_shape=[jax.ShapeDtyp...  49.4 us
    pallas_call x1, Pallas kernels, per_device(): pl.pallas_call(hand_over, out_shape=[jax.ShapeDtypeStruct((cx, cz, ny), f...  1.91 us

profile of v2, /device:TPU:57, one launch (start us, length us, event | category | flops | bytes accessed | tf_op | source)
XLA Modules:
  0.0 52.6 jit_solution(2816087234305318616)
XLA Ops:
  1.3 49.4 %leapfrog.1 = (f32[16,16,512]{2,1,0:T(8,128)}, f32[256,128]{1,0:T(8,128)}) custom-call(f32[16,16,512]{2,1,0:T(8,128)} %p_hbm.1, f32[16,16,512]{2,1,0:T(8,128)} %q_hbm.1, f32[256,128]{1,0:T(8,128)} %bitcast.5, s32[1,256]{1,0:T(1,128)} %bitcast.6, s32[1,1]{1,0:T(1,128)S(6)} %copy.12.count_ref, s32[1,256]{1,0:T(1,128)} %bitcast.7, s32[1,256]{1,0:T(1,128)} %bitcast.8, ...), custom_call_target="tpu_custom_call" | custom-call | tf_op jit(solution)/shard_map/leapfrog/pallas_call | solution.py:599
  50.7 1.9 %hand_over.1 = (f32[16,16,512]{2,1,0:T(8,128)}, f32[256,128]{1,0:T(8,128)}) custom-call(f32[16,16,512]{2,1,0:T(8,128)} %get-tuple-element.6.p_ref, f32[256,128]{1,0:T(8,128)} %get-tuple-element.7.s_ref), custom_call_target="tpu_custom_call" | custom-call | tf_op jit(solution)/shard_map/hand_over/pallas_call | solution.py:671

commit v3 on v2

--- a/solution.py
+++ b/solution.py
@@ -10,8 +10,7 @@
 MESH = pl.DeviceIdType.MESH
 STEPS = 3
 CHUNKS = 2
-PRESSURE_AT = (0, 1, 1)
-SEND_ORDER = 2
+PRESSURE_AT = (1, 1, 1)
 OTHER, BEFORE, AFTER = range(3)
 OWN, MIRROR = range(2)
 
@@ -204,9 +203,11 @@
     def plane_at(t, x):
         return pressure.at[0, x + 1] if t == 0 else free.at[t - 1, x]
 
-    def p_copies(t):
+    def p_copies(t, ways=None):
         copies = []
         for (dx, dz), (present, device) in near.items():
+            if ways is not None and (-dx, -dz) not in ways:
+                continue
             k = order[dx, dz]
             if dz == 0:
                 src = plane_at(t, cx - 1 if dx > 0 else 0)
@@ -222,21 +223,28 @@
             )
         return copies
 
-    def send_faces(t):
-        for x in range(cx):
-            here = plane_at(t, x)
-            face_z[t, 0, x : x + 1, :] = here[0:1, :]
-            face_z[t, 1, x : x + 1, :] = here[cz - 1 : cz, :]
-        for (dx, dz), k in corner_of.items():
-            here = plane_at(t, cx - 1 if dx > 0 else 0)
-            z = cz - 1 if dz > 0 else 0
-            face_c[t, k] = here[z : z + 1, :]
-        for goes, _, copy in p_copies(t):
+    along_z = [way for way in order if way[0] == 0]
+    along_x = [way for way in order if way[0] != 0]
+
+    def send_faces(t, ways):
+        if ways == along_z:
+            for x in range(cx):
+                here = plane_at(t, x)
+                face_z[t, 0, x : x + 1, :] = here[0:1, :]
+                face_z[t, 1, x : x + 1, :] = here[cz - 1 : cz, :]
+        else:
+            for (dx, dz), k in corner_of.items():
+                here = plane_at(t, cx - 1 if dx > 0 else 0)
+                z = cz - 1 if dz > 0 else 0
+                face_c[t, k] = here[z : z + 1, :]
+        for goes, _, copy in p_copies(t, ways):
             pl.when(goes)(copy.start)
 
-    def e_copies(t):
+    def e_copies(t, ways=None):
         copies = []
         for (dx, dz), (present, device) in near.items():
+            if ways is not None and (-dx, -dz) not in ways:
+                continue
             k = order[dx, dz]
             copy = remote(
                 edge_out.at[t],
@@ -282,18 +290,11 @@
         for c in range(CHUNKS):
             send_state(0, OWN, c)
 
-    if SEND_ORDER == 2:
-        loads[1].wait()
-        send_faces(0)
+    loads[1].wait()
+    send_faces(0, along_x)
+    send_faces(0, along_z)
     for c in range(CHUNKS):
         cross(c).start()
-    if SEND_ORDER == 0:
-        send_own()
-    if SEND_ORDER <= 1:
-        loads[1].wait()
-        send_faces(0)
-    if SEND_ORDER == 1:
-        send_own()
     for k, load in enumerate(loads):
         if k > 1:
             load.wait()
@@ -309,13 +310,13 @@
     about.start()
 
     along = lax.rem(cell_ref[...], ny).astype(jnp.float32)
-    column[...] = jnp.transpose(jnp.broadcast_to(along, (lanes, slots)))
+    column[0] = jnp.transpose(jnp.broadcast_to(along, (lanes, slots)))
     send_edges(0, along)
     lane = lax.broadcasted_iota(jnp.int32, (cz, lanes), 1).astype(jnp.float32)
     for x in range(cx):
         for part in range(parts):
             mask[x, :, part * lanes : (part + 1) * lanes] = (
-                column[x * cz : (x + 1) * cz] == lane + float(part * lanes)
+                column[0, x * cz : (x + 1) * cz] == lane + float(part * lanes)
             ).astype(jnp.float32)
 
     in_t = jnp.transpose(jnp.concatenate([input_ref[...], output_ref[...]], axis=0))
@@ -391,19 +392,15 @@
         along_y = lax.broadcasted_iota(jnp.int32, (place.shape[0], ny), 1).astype(jnp.float32)
         return jnp.where(place == along_y, value, 0.0)
 
-    along_z = [way for way in order if way[0] == 0]
-    along_x = [way for way in order if way[0] != 0]
-
     def wait_for(t, ways):
-        copies = p_copies(t)
-        if t > 0:
-            copies += e_copies(t)
-        for n, (_, comes, copy) in enumerate(copies):
-            if list(order)[n % 8] in ways:
-                pl.when(comes)(copy.wait_recv)
+        for _, comes, copy in p_copies(t, ways) + (e_copies(t, ways) if t > 0 else []):
+            pl.when(comes)(copy.wait_recv)
 
     def pressure_free(t):
         last = t + 1 == STEPS
+        if t > 0:
+            for x in range(cx):
+                pressure[t, x + 1] = free[t - 1, x] - column[t - 1, x * cz : (x + 1) * cz, 0:1] * mask[x]
 
         def inside(x):
             return both_z(pressure[t, x + 1], halo_z[t, 0, pl.ds(x, 1), :], halo_z[t, 1, pl.ds(x, 1), :])
@@ -416,7 +413,7 @@
             total = both_y(even + rest_w * mid) + even + rest_w * (here + beside) + (centre_w - edge_w) * mid
             value = 2.0 * mid - past + courant * total
             if last:
-                free[t, x] = value - column[pl.ds(x * cz, cz), 0:1] * mask[x]
+                free[t, x] = value - column[t, pl.ds(x * cz, cz), 0:1] * mask[x]
             else:
                 free[t, x] = value
                 pick(x, value - mid)
@@ -436,28 +433,36 @@
             turn_edges(t, 1, along_z)
             for end in (0, 1):
                 halo_z[t, end] -= spread((0, 2 * end - 1))
-        before, here = lax.fori_loop(1, cx - 1, step, (inside(0), inside(1)), unroll=2)
+        def inner():
+            lax.fori_loop(1, cx - 1, step, (inside(0), inside(1)), unroll=2)
+
+        def outer():
+            wait_for(t, along_x)
+            if t > 0:
+                turn_edges(t, 2, along_x)
+                for end in (0, 1):
+                    side = 2 * end - 1
+                    pressure[t, end * (cx + 1)] -= spread((side, 0))
+                    for z in (-1, 1):
+                        halo_c[t, corner_of[side, z]] -= spread((side, z))
+            ends = []
+            for end in (0, 1):
+                at = [halo_c[t, corner_of[2 * end - 1, z]] for z in (-1, 1)]
+                ends.append(both_z(pressure[t, end * (cx + 1)], *at))
+            one(0, ends[0], inside(0), inside(1))
+            one(cx - 1, inside(cx - 2), inside(cx - 1), ends[1])
+
         if last:
+            inner()
             stores[1].start()
-        wait_for(t, along_x)
-        if t > 0:
-            turn_edges(t, 2, along_x)
-            for end in (0, 1):
-                side = 2 * end - 1
-                pressure[t, end * (cx + 1)] -= spread((side, 0))
-                for z in (-1, 1):
-                    halo_c[t, corner_of[side, z]] -= spread((side, z))
-
-        def ends(end):
-            at = [halo_c[t, corner_of[2 * end - 1, z]] for z in (-1, 1)]
-            return both_z(pressure[t, end * (cx + 1)], *at)
-
-        one(cx - 1, before, here, ends(1))
-        one(0, ends(0), inside(0), inside(1))
-        if last:
+            outer()
             stores[2].start()
             stores[3].start()
             return None
+        outer()
+        send_faces(t + 1, along_x)
+        inner()
+        send_faces(t + 1, along_z)
         return picked_row()
 
     def gathered(side, d, value):
@@ -477,7 +482,7 @@
         base[side] = total + coupling * (own[:filt] + own[filt:] - now)
 
     def across(side, t):
-        base[side] += velocity[side] * drive[side] + coupling * gathered(side, 1, state[1 - side, t])
+        base[side] += coupling * gathered(side, 1, state[1 - side, t])
 
     def do_pressure(t):
         change = pressure_free(t)
@@ -486,7 +491,6 @@
         if t + 2 < STEPS:
             v_out[t + 1] = change
             v_copy(t + 1).start()
-        send_faces(t + 1)
         return change
 
     def come(side, t):
@@ -499,8 +503,7 @@
             if t + 1 < STEPS and (c + 1 < CHUNKS or side == MIRROR):
                 send_state(t + 1, side, c)
 
-    if SEND_ORDER == 2:
-        send_own()
+    send_own()
     mixed(OWN, 0)
     for c in range(CHUNKS):
         cross(c).wait_recv()
@@ -513,6 +516,10 @@
         if t > 0:
             mixed(OWN, t)
         across(OWN, t)
+        base[OWN] += velocity[OWN] * drive[OWN]
+        if t == 1:
+            mixed(MIRROR, t)
+            across(MIRROR, t)
         if PRESSURE_AT[t] == 0:
             change = do_pressure(t)
         come(OWN, t)
@@ -524,21 +531,20 @@
         else:
             s_ref[...] = jnp.transpose(state[OWN, STEPS])
             stores[0].start()
-        column[...] = jnp.broadcast_to(jnp.sum(jnp.transpose(product), axis=1, keepdims=True), (slots, lanes))
+        column[t] = jnp.broadcast_to(jnp.sum(jnp.transpose(product), axis=1, keepdims=True), (slots, lanes))
         if PRESSURE_AT[t] == 1:
             change = do_pressure(t)
         if t + 1 < STEPS:
-            mixed(MIRROR, t)
+            if t == 0:
+                mixed(MIRROR, t)
+                across(MIRROR, t)
             v_copy(t).wait_recv()
-            velocity[MIRROR] = v_in[t] - (behind if t > 0 else 0.0)
-            across(MIRROR, t)
+            base[MIRROR] += (v_in[t] - (behind if t > 0 else 0.0)) * drive[MIRROR]
             come(MIRROR, t)
             behind = jnp.sum(state[MIRROR, t + 1] * readout[MIRROR], axis=0, keepdims=True)
             if PRESSURE_AT[t] == 2:
                 change = do_pressure(t)
             velocity[OWN] = change - correction
-            for x in range(cx):
-                pressure[t + 1, x + 1] = free[t, x] - column[x * cz : (x + 1) * cz, 0:1] * mask[x]
 
     for store in stores:
         store.wait()
@@ -635,7 +641,7 @@
             pltpu.VMEM((STEPS, 1, slots), f32),
             pltpu.VMEM((STEPS, 8, 1, slots), f32),
             pltpu.VMEM((3, slots, 128), f32),
-            pltpu.VMEM((slots, 128), f32),
+            pltpu.VMEM((STEPS, slots, 128), f32),
             pltpu.VMEM((STEPS, cx, cz, ny), f32),
             pltpu.VMEM((slots, 128), f32),
             pltpu.SemaphoreType.DMA((9,)),

time: 52.7 us -> 52.6 us (level)
  the two profiles are of different devices: /device:TPU:57 before, /device:TPU:14 now
where the time goes in v3:
time: 52.6 us; the launch traced here: 52.4 us
  Pallas kernels  51.2 us (97%)
  between operations  1.29 us (2%)
    pallas_call x1, Pallas kernels, per_device(): pl.pallas_call(functools.partial(kernel, sizes), out_shape=[jax.ShapeDtyp...  49.2 us
    pallas_call x1, Pallas kernels, per_device(): pl.pallas_call(hand_over, out_shape=[jax.ShapeDtypeStruct((cx, cz, ny), f...  1.91 us

profile of v3, /device:TPU:14, one launch (start us, length us, event | category | flops | bytes accessed | tf_op | source)
XLA Modules:
  0.0 52.4 jit_solution(6948379917900851713)
XLA Ops:
  1.3 49.2 %leapfrog.1 = (f32[16,16,512]{2,1,0:T(8,128)}, f32[256,128]{1,0:T(8,128)}) custom-call(f32[16,16,512]{2,1,0:T(8,128)} %p_hbm.1, f32[16,16,512]{2,1,0:T(8,128)} %q_hbm.1, f32[256,128]{1,0:T(8,128)} %bitcast.5, s32[1,256]{1,0:T(1,128)} %bitcast.6, s32[1,1]{1,0:T(1,128)S(6)} %copy.12.count_ref, s32[1,256]{1,0:T(1,128)} %bitcast.7, s32[1,256]{1,0:T(1,128)} %bitcast.8, ...), custom_call_target="tpu_custom_call" | custom-call | tf_op jit(solution)/shard_map/leapfrog/pallas_call | solution.py:605
  50.5 1.9 %hand_over.1 = (f32[16,16,512]{2,1,0:T(8,128)}, f32[256,128]{1,0:T(8,128)}) custom-call(f32[16,16,512]{2,1,0:T(8,128)} %get-tuple-element.6.p_ref, f32[256,128]{1,0:T(8,128)} %get-tuple-element.7.s_ref), custom_call_target="tpu_custom_call" | custom-call | tf_op jit(solution)/shard_map/hand_over/pallas_call | solution.py:677
